TPU v7x, 32 devices: a whole 2x2x4 slice. The times are simulated.
32 devices in a mesh: band: 8 (over z, x), lev: 4 (over y, core).
Axes of the slice: x: 2, y: 2, z: 4, core: 2. Of those that a mesh axis runs over, the one named last changes fastest.
Arguments:
- temp_spectrum: bfloat16 [160, 1280, 2, 136], P('band', None, None, 'lev'), may hold values from -0.875 to 0.875
- surf_spectrum: bfloat16 [160, 1280, 2], P('band'), may hold values from -0.875 to 0.875
- legendre: bfloat16 [160, 16, 1280], P('band'), may hold values from -0.15625 to 0.15625
- m_order: int32 [160], replicated, may hold values from 0 to 159, each once
- hydro_matrix: bfloat16 [136, 136], P('lev'), may hold values from 0.029907227 to 0.29882812
- surf_coupling: float32 [136], P('lev'), may hold values from 0.3 to 3
- src_blocks: int32 [640, 4], P('band'), may hold values from 0 to 639, as said below
- tap_index: int32 [640, 4, 128], P('band'), may hold values from 0 to 511
- tap_weight: float32 [640, 4, 128], P('band'), may hold values from 0.05 to 0.45
Outputs:
- departed: float32 [16, 136, 5120], P('band', 'lev')
Inputs may be any that keep to these rules, and one draw needn't show every extreme that they name: `src_blocks`: slots 0 and 2 of a reader block name blocks of the reader's own band device, slot 1 a block of the device before it and slot 3 a block of the device after it, or of the reader's own device where that neighbour does not exist. The readers of one device name at most 16 distinct blocks of each neighbour, and some device names exactly 16 of one neighbour.
All inputs are finite; a program needn't handle non-finite values.
Results may differ from a plain program's by a relative error of at most 0.0047.
Values may be sent and summed in bfloat16 or wider, within the bound.
A program may use at most 128 MiB of HBM per device.

v0:
```python
import functools
import math

import jax
import jax.numpy as jnp
from jax import lax
from jax.experimental import pallas as pl
from jax.experimental.pallas import tpu as pltpu
from jax.sharding import PartitionSpec as P

NLON = 5120
BLK = 128
SLOTS = 4
TAPS = 4
XB = NLON // BLK
SP = 24
RS = 2 * SP
LR = 48
KP = 40
JJ = 6
WIDE = 256
MESH = pl.DeviceIdType.MESH


def exchange_kernel(nb, nl, f_ref, h_ref, s_ref, out_ref, fall, ft, pieces, h, sa, ra, sb, rb):
    band = lax.axis_index("band")
    lev = lax.axis_index("lev")
    barrier = pltpu.get_barrier_semaphore()

    def greet_lev(i, _):
        pl.semaphore_signal(
            barrier, inc=1, device_id=(band, lax.rem(lev + i, nl)), device_id_type=MESH
        )
        return 0

    def greet_band(i, _):
        pl.semaphore_signal(
            barrier, inc=1, device_id=(lax.rem(band + i, nb), lev), device_id_type=MESH
        )
        return 0

    lax.fori_loop(1, nl, greet_lev, 0)
    lax.fori_loop(1, nb, greet_band, 0)
    pl.semaphore_wait(barrier, nl - 1 + nb - 1)

    def copy_a(i):
        peer = lax.rem(lev + i, nl)
        return pltpu.make_async_remote_copy(
            src_ref=f_ref,
            dst_ref=fall.at[lev],
            send_sem=sa.at[i],
            recv_sem=ra.at[i],
            device_id=(band, peer),
            device_id_type=MESH,
        )

    for i in range(1, nl):
        copy_a(i).start()
    width = f_ref.shape[1]
    edge = 2 * RS
    zero = jnp.zeros((edge + RS, nl * LR), jnp.bfloat16)
    lev_dev, lev_total = h_ref.shape
    row = lax.broadcasted_iota(jnp.int32, (lev_dev, lev_total), 0) + lev * lev_dev
    col = lax.broadcasted_iota(jnp.int32, (lev_dev, lev_total), 1)
    upper = jnp.where(col >= row, h_ref[...].astype(jnp.float32), 0.0).astype(jnp.bfloat16)
    row = lax.broadcasted_iota(jnp.int32, (nl * LR, lev_total), 0)
    col = lax.broadcasted_iota(jnp.int32, (nl * LR, lev_total), 1)
    spots = jnp.zeros((nl * LR, lev_total), jnp.float32)
    for v in range(nl):
        inside = (row >= v * LR) & (row < v * LR + lev_dev)
        spots = jnp.where(inside & (col == row - v * (LR - lev_dev)), 1.0, spots)
    tall = lax.dot_general(
        spots.astype(jnp.bfloat16),
        upper,
        (((1,), (1,)), ((), ())),
        preferred_element_type=jnp.float32,
    )
    row = lax.broadcasted_iota(jnp.int32, (nl * LR, lev_dev), 0)
    surf = jnp.broadcast_to(s_ref[...], (nl * LR, lev_dev))
    tall = jnp.where(row == lev * LR + lev_dev, surf, tall).astype(jnp.bfloat16)
    row = lax.broadcasted_iota(jnp.int32, (lev_dev, WIDE), 0)
    col = lax.broadcasted_iota(jnp.int32, (lev_dev, WIDE), 1)
    for jj in range(JJ):
        place = jnp.where(col == row + jj * KP, 1.0, 0.0).astype(jnp.bfloat16)
        h[jj] = jnp.dot(tall, place, preferred_element_type=jnp.float32).astype(jnp.bfloat16)
    ft[0:edge, :] = zero[:edge]
    ft[edge + width : edge + width + edge + RS, :] = zero
    fall[lev] = f_ref[...]
    for i in range(1, nl):
        copy_a(i).wait()
    step = 768
    for c in range(0, width, step):
        part = fall[:, :, c : c + step].reshape(nl * LR, step).astype(jnp.float32)
        ft[edge + c : edge + c + step, :] = part.T.astype(jnp.bfloat16)

    batch = math.gcd(nb, 8)
    span = batch * 2 * RS

    def make(g, _):
        total = jnp.zeros((batch * RS, WIDE), jnp.float32)
        for jj in range(JJ):
            rows = ft[pl.ds(pl.multiple_of(g * span + jj * RS, 16), span), :]
            rows = rows.reshape(batch, 2 * RS, nl * LR)[:, :RS].reshape(batch * RS, nl * LR)
            total = total + jnp.dot(rows, h[jj], preferred_element_type=jnp.float32)
        pieces[pl.ds(g * batch, batch)] = total.astype(jnp.bfloat16).reshape(batch, RS, WIDE)
        return 0

    lax.fori_loop(0, nb // batch, make, 0)

    def copy_b(i):
        peer = lax.rem(band + i, nb)
        return pltpu.make_async_remote_copy(
            src_ref=pieces.at[peer],
            dst_ref=out_ref.at[band],
            send_sem=sb.at[i],
            recv_sem=rb.at[i],
            device_id=(peer, lev),
            device_id_type=MESH,
        )

    def send(i, _):
        copy_b(i).start()
        return 0

    lax.fori_loop(1, nb, send, 0)
    out_ref[band] = pieces[band]

    def done(i, _):
        copy_b(i).wait()
        return 0

    lax.fori_loop(1, nb, done, 0)


def exchange(f, h, s, nb, nl):
    width = f.shape[1]
    vmem = pl.BlockSpec(memory_space=pltpu.VMEM)
    return pl.pallas_call(
        functools.partial(exchange_kernel, nb, nl),
        out_shape=jax.ShapeDtypeStruct((nb, RS, WIDE), jnp.bfloat16),
        in_specs=[vmem, vmem, vmem],
        out_specs=vmem,
        scratch_shapes=[
            pltpu.VMEM((nl, LR, width), jnp.bfloat16),
            pltpu.VMEM((width + 5 * RS, nl * LR), jnp.bfloat16),
            pltpu.VMEM((nb, RS, WIDE), jnp.bfloat16),
            pltpu.VMEM((JJ, nl * LR, WIDE), jnp.bfloat16),
            pltpu.SemaphoreType.DMA((nl,)),
            pltpu.SemaphoreType.DMA((nl,)),
            pltpu.SemaphoreType.DMA((nb,)),
            pltpu.SemaphoreType.DMA((nb,)),
        ],
        compiler_params=pltpu.CompilerParams(
            collective_id=0, has_side_effects=True, vmem_limit_bytes=41943040
        ),
    )(f, h, s)


def angle(phase):
    phase = phase - NLON * jnp.floor(phase * (1.0 / NLON))
    return phase * (2.0 * math.pi / NLON)


def grid_kernel(nb, lev_dev, src_ref, coef_ref, wave_ref, idx_ref, wgt_ref, out_ref, table, pool):
    pair = math.gcd(nb, 2)
    tall = pair * SP

    def build(b, _):
        rows = pl.ds(pl.multiple_of(b * tall, 8), tall)
        orders = jnp.broadcast_to(wave_ref[rows, :], (tall, BLK))
        points = lax.broadcasted_iota(jnp.int32, (tall, BLK), 1).astype(jnp.float32)
        start, turn = angle(orders * points), angle(orders * float(BLK))
        factor = jnp.where(orders < 0.0, 0.0, jnp.where(orders == 0.0, 1.0, 2.0))
        real, imag = factor * jnp.cos(start), factor * jnp.sin(start)
        turn_c, turn_s = jnp.cos(turn), jnp.sin(turn)
        place = pl.ds(pl.multiple_of(b * pair * RS, 16), pair * RS)
        for x in range(XB):
            parts = []
            for u in range(pair):
                own = slice(u * SP, (u + 1) * SP)
                parts += [real[own], -imag[own]]
            both = jnp.concatenate(parts, axis=0)
            table[place, x * BLK : (x + 1) * BLK] = both.astype(jnp.bfloat16)
            real, imag = real * turn_c - imag * turn_s, imag * turn_c + real * turn_s
        return 0

    lax.fori_loop(0, nb // pair, build, 0)
    coef = coef_ref[...].reshape(nb * RS, WIDE).astype(jnp.float32).T.astype(jnp.bfloat16)
    group = 4

    def synth(c, _):
        cols = pl.ds(pl.multiple_of(c * (group * BLK), 128), group * BLK)
        grid = jnp.dot(coef, table[:, cols], preferred_element_type=jnp.float32)
        for jj in range(JJ):
            for g in range(group):
                pool[jj * XB + c * group + g] = grid[
                    jj * KP : (jj + 1) * KP, g * BLK : (g + 1) * BLK
                ]
        return 0

    lax.fori_loop(0, XB // group, synth, 0)
    half = 2 * BLK
    cells = lax.broadcasted_iota(jnp.int32, (half, BLK), 0).astype(jnp.bfloat16)
    zero = jnp.zeros((half, BLK), jnp.bfloat16)

    first = (lax.axis_index("band") - 1) * (2 * XB)

    def read(b):
        idx = idx_ref[b]
        wgt = wgt_ref[b].astype(jnp.bfloat16)
        total = None
        for h in range(2):
            spot = (idx - h * half).astype(jnp.float32).astype(jnp.bfloat16)
            spread = zero
            for t in range(TAPS):
                hit = cells == jnp.broadcast_to(spot[t : t + 1, :], (half, BLK))
                spread = spread + jnp.where(
                    hit, jnp.broadcast_to(wgt[t : t + 1, :], (half, BLK)), zero
                )
            source = jnp.concatenate(
                [pool[src_ref[2 * h, b] - first], pool[src_ref[2 * h + 1, b] - first]], axis=1
            ).astype(jnp.bfloat16)
            part = jnp.dot(source, spread, preferred_element_type=jnp.float32)
            total = part if total is None else total + part
        return total

    for j in range(2):

        def step(x, _):
            for u in range(8):
                xb = x * 8 + u
                out_ref[:, j, pl.ds(pl.multiple_of(xb * BLK, 128), BLK)] = read(j * XB + xb)[
                    :lev_dev
                ]
            return 0

        lax.fori_loop(0, XB // 8, step, 0)


def grid_part(src, coef, wave, idx, wgt, nb, lev_dev):
    vmem = pl.BlockSpec(memory_space=pltpu.VMEM)
    return pl.pallas_call(
        functools.partial(grid_kernel, nb, lev_dev),
        out_shape=jax.ShapeDtypeStruct((lev_dev, 2, NLON), jnp.float32),
        in_specs=[pl.BlockSpec(memory_space=pltpu.SMEM)] + [vmem] * 4,
        out_specs=vmem,
        scratch_shapes=[
            pltpu.VMEM((nb * RS, NLON), jnp.bfloat16),
            pltpu.VMEM((JJ * XB, KP, BLK), jnp.float32),
        ],
        compiler_params=pltpu.CompilerParams(vmem_limit_bytes=58720256),
    )(src, coef, wave, idx, wgt)


def waves(m_order, nb, slots):
    orders = m_order.astype(jnp.float32).reshape(nb, slots)
    orders = jnp.pad(orders, ((0, 0), (0, SP - slots)), constant_values=-1.0)
    return orders.reshape(nb * SP, 1)


def shards(
    temp_spectrum,
    surf_spectrum,
    legendre,
    m_order,
    hydro_matrix,
    surf_coupling,
    src_blocks,
    tap_index,
    tap_weight,
):
    slots, n_count, _, lev_dev = temp_spectrum.shape
    lat_all = legendre.shape[1]
    nb, nl = lax.axis_size("band"), lax.axis_size("lev")
    band = lax.axis_index("band")
    my_orders = lax.dynamic_slice_in_dim(m_order, band * slots, slots)
    n_index = jnp.arange(n_count, dtype=jnp.int32)
    keep = n_index[None, None, :] >= my_orders[:, None, None]
    values = jnp.where(keep, legendre, jnp.zeros_like(legendre))
    four_t = jnp.einsum(
        "sjn,snrk->sjrk", values, temp_spectrum, preferred_element_type=jnp.float32
    ).astype(jnp.bfloat16)
    four_p = jnp.einsum(
        "sjn,snr->sjr", values, surf_spectrum, preferred_element_type=jnp.float32
    ).astype(jnp.bfloat16)
    four = jnp.concatenate([four_t, four_p[..., None]], axis=3)
    four = jnp.transpose(four, (3, 1, 2, 0))
    four = jnp.pad(four, ((0, LR - lev_dev - 1), (0, 0), (0, 0), (0, SP - slots)))
    four = four.reshape(LR, lat_all * RS)

    coef = exchange(four, hydro_matrix, surf_coupling[None, :], nb, nl)
    out = grid_part(
        src_blocks.T, coef, waves(m_order, nb, slots), tap_index, tap_weight, nb, lev_dev
    )
    return jnp.transpose(out, (1, 0, 2))


def solution(mesh):
    in_specs = (
        P("band", None, None, "lev"),
        P("band", None, None),
        P("band", None, None),
        P(),
        P("lev", None),
        P("lev"),
        P("band", None),
        P("band", None, None),
        P("band", None, None),
    )
    out_specs = P("band", "lev", None)
    return jax.shard_map(shards, mesh=mesh, in_specs=in_specs, out_specs=out_specs, check_vma=False)
```

profile of v0, /device:TPU:0, one launch (start us, length us, event | category | flops | bytes accessed | tf_op | source)
XLA Modules:
  0.0 44.7 jit_solution(5599944503410359345)
XLA Ops:
  0.0 0.0 copy-start
  0.0 0.9 %dynamic_slice.3 = s32[20]{0:T(128)S(1)} dynamic-slice(s32[160]{0:T(256)} %param.12, s32[]{:T(128)S(6)} %select_n.7), dynamic_slice_sizes={20} | dynamic-slice | bytes 164 | tf_op jit(solution)/shard_map/dynamic_slice | solution.py:276
  0.9 0.8 %convert_element_type.13 = f32[160]{0:T(256)S(1)} convert(s32[160]{0:T(256)} %param.12) | non-fusion elementwise | flops 160 | bytes 1280 | tf_op jit(solution)/shard_map/convert_element_type | solution.py:256
  1.7 0.1 reshape.31
  1.8 0.1 iota_compare_fusion
  1.9 1.5 %fusion.5 = bf16[20,16,2,1]{1,2,0,3:T(2,128)(2,1)S(1)} fusion(bf16[20,1280,2]{1,2,0:T(2,128)(2,1)} %param.10, bf16[20,16,1280]{2,1,0:T(8,128)(2,1)} %param.11, pred[20,1280]{1,0:T(8,128)(4,1)S(1)} %iota_compare_fusion), kind=kOutput, calls=%fused_computation.4 | convolution fusion | flops 2048640 | bytes 948480 | tf_op jit(solution)/shard_map/sjn,snr->sjr/dot_general | solution.py:283
  3.5 0.7 %reshape.34.wave_ref = f32[192,1]{1,0:T(8,128)} reshape(f32[8,24]{1,0:T(8,128)S(1)} %pad.9) | data formatting | bytes 1536 | tf_op jit(solution)/shard_map/reshape | solution.py:258
  4.2 0.0 copy-done
  4.2 4.1 %fusion.2 = bf16[20,16,2,34]{3,1,2,0:T(8,128)(2,1)} fusion(bf16[20,1280,2,34]{1,2,3,0:T(2,128)(2,1)S(1)} %copy-done, bf16[20,16,1280]{2,1,0:T(8,128)(2,1)} %param.11, pred[20,1280]{1,0:T(8,128)(4,1)S(1)} %iota_compare_fusion), kind=kOutput, calls=%fused_computation.2 | convolution fusion | flops 56136960 | bytes 4369920 | tf_op jit(solution)/shard_map/sjn,snrk->sjrk/dot_general | solution.py:280
  8.4 1.0 %copy.14 = bf16[20,16,2,1]{3,1,2,0:T(8,128)(2,1)} copy(bf16[20,16,2,1]{1,2,0,3:T(2,128)(2,1)S(1)} %fusion.5) | data formatting | bytes 2560 | tf_op jit(solution)/shard_map/broadcast_in_dim | solution.py:286
  9.3 1.1 %maximum_bitcast_fusion = bf16[35,16,2,20]{0,1,2,3:T(8,128)(2,1)S(1)} fusion(bf16[20,16,2,1]{3,1,2,0:T(8,128)(2,1)} %copy.14, bf16[20,16,2,34]{3,1,2,0:T(8,128)(2,1)} %fusion.2), kind=kLoop, calls=%fused_computation.9 | loop fusion | flops 89600 | bytes 89600 | tf_op jit(solution)/shard_map/transpose | solution.py:287
  10.5 0.1 copy.21
  10.5 0.7 %pad.8.clone = bf16[48,16,2,24]{0,3,2,1:T(8,128)(2,1)} pad(bf16[35,16,2,20]{0,3,2,1:T(8,128)(2,1)S(1)} %copy.21, bf16[]{:T(256)} %constant.15.clone.1), padding=0_13x0_0x0_0x0_4 | pad | bytes 118530 | tf_op jit(solution)/shard_map/jit(_pad)/pad | solution.py:288
  11.3 1.0 %copy.16.f_ref = bf16[48,768]{1,0:T(8,128)(2,1)S(1)} copy(bf16[48,768]{0,1:T(8,128)(2,1)} %bitcast.15) | data formatting | bytes 147456 | tf_op jit(solution)/shard_map/reshape | solution.py:289
  12.3 0.0 copy-start.2
  12.3 0.7 %copy-done.2 = bf16[34,136]{1,0:T(8,128)(2,1)S(1)} copy-done((bf16[34,136]{1,0:T(8,128)(2,1)S(1)}, bf16[34,136]{1,0:T(8,128)(2,1)}, u32[]{:S(2)}) %copy-start.2) | copy-done | bytes 9272
  13.0 0.0 copy-start.3
  13.0 0.7 %copy-done.3 = f32[34]{0:T(128)S(1)} copy-done((f32[34]{0:T(128)S(1)}, f32[34]{0:T(128)}, u32[]{:S(2)}) %copy-start.3) | copy-done | bytes 160
  13.7 15.9 %shard_map.91.coef_ref = bf16[8,48,256]{2,1,0:T(8,128)(2,1)S(1)} custom-call(bf16[48,768]{1,0:T(8,128)(2,1)S(1)} %copy.16.f_ref, bf16[34,136]{1,0:T(8,128)(2,1)S(1)} %copy-done.2, f32[1,34]{1,0:T(1,128)S(1)} %bitcast.14), custom_call_target="tpu_custom_call" | custom-call | tf_op jit(solution)/shard_map/pallas_call | solution.py:138
  29.6 0.0 copy-start.1
  29.6 0.7 %copy-done.1 = bf16[8,48,256]{2,1,0:T(8,128)(2,1)} copy-done((bf16[8,48,256]{2,1,0:T(8,128)(2,1)}, bf16[8,48,256]{2,1,0:T(8,128)(2,1)S(1)}, u32[]{:S(2)}) %copy-start.1) | copy-done | bytes 196632
  30.2 14.5 %shard_map.92 = f32[34,2,5120]{2,1,0:T(2,128)} custom-call(s32[4,80]{1,0:T(4,128)} %bitcast.16, bf16[8,48,256]{2,1,0:T(8,128)(2,1)} %copy-done.1, f32[192,1]{1,0:T(8,128)} %reshape.34.wave_ref, s32[80,4,128]{2,1,0:T(4,128)} %idx_ref.1, f32[80,4,128]{2,1,0:T(4,128)} %wgt_ref.1), custom_call_target="tpu_custom_call" | custom-call | tf_op jit(solution)/shard_map/pallas_call | solution.py:242
  (1 shorter events, 0.0 us)
Async XLA Ops:
  0.0 4.2 %copy-start = (bf16[20,1280,2,34]{1,2,3,0:T(2,128)(2,1)S(1)}, bf16[20,1280,2,34]{1,2,3,0:T(2,128)(2,1)}, u32[]{:S(2)}) copy-start(bf16[20,1280,2,34]{1,2,3,0:T(2,128)(2,1)} %param.9) | copy-start | bytes 10444804
  12.3 0.7 %copy-start.2 = (bf16[34,136]{1,0:T(8,128)(2,1)S(1)}, bf16[34,136]{1,0:T(8,128)(2,1)}, u32[]{:S(2)}) copy-start(bf16[34,136]{1,0:T(8,128)(2,1)} %h_ref.1) | copy-start | bytes 27748
  13.0 0.7 %copy-start.3 = (f32[34]{0:T(128)S(1)}, f32[34]{0:T(128)}, u32[]{:S(2)}) copy-start(f32[34]{0:T(128)} %param.14) | copy-start | bytes 412
  29.6 0.7 %copy-start.1 = (bf16[8,48,256]{2,1,0:T(8,128)(2,1)}, bf16[8,48,256]{2,1,0:T(8,128)(2,1)S(1)}, u32[]{:S(2)}) copy-start(bf16[8,48,256]{2,1,0:T(8,128)(2,1)S(1)} %shard_map.91.coef_ref) | copy-start | bytes 589828
where the time goes:
time: 45 us; the launch traced here: 44.7 us
  Pallas kernels  30.3 us (67%)
  local copies, waits for them, and re-layouts  6.59 us (15%)
  matrix products  5.69 us (13%)
  other arithmetic  2.04 us (5%)
    pallas_call x1, Pallas kernels, exchange(): pl.pallas_call(functools.partial(exchange_kernel, nb, nl), out_shape=jax....  15.9 us
    pallas_call x1, Pallas kernels, grid_part(): pl.pallas_call(functools.partial(grid_kernel, nb, lev_dev), out_shape=jax...  14.5 us
    dot_general x1, matrix products, shards(): jnp.einsum('sjn,snrk->sjrk', values, temp_spectrum, preferred_element_typ...  4.15 us
    unnamed x9, local copies, waits for them, and re-layouts  2.12 us
    dot_general x1, matrix products, shards(): jnp.einsum('sjn,snr->sjr', values, surf_spectrum, preferred_element_type=...  1.54 us
    transpose x1, other arithmetic, shards(): four = jnp.transpose(four, (3, 1, 2, 0))  1.11 us
    reshape x1, local copies, waits for them, and re-layouts, shards(): four = four.reshape(LR, lat_all * RS)  1.04 us
    broadcast_in_dim x1, local copies, waits for them, and re-layouts, shards(): four = jnp.concatenate([four_t, four_p[..., None]], axis=3)  0.98 us

commit v1 on v0

v1 whole, which is shorter than its diff:
```python
import functools
import math

import jax
import jax.numpy as jnp
from jax import lax
from jax.experimental import pallas as pl
from jax.experimental.pallas import tpu as pltpu
from jax.sharding import PartitionSpec as P

NLON = 5120
BLK = 128
TAPS = 4
XB = NLON // BLK
S = 20
CHUNKS = ((0, 8), (8, 8), (16, 4))
LOAD = 4
KP = 40
PR = 40
JJ = 6
HALF = 256
LATE = 58
MESH = pl.DeviceIdType.MESH
BF = jnp.bfloat16
F32 = jnp.float32


def iota(shape, dim):
    return lax.broadcasted_iota(jnp.int32, shape, dim)


def cosine(steps):
    steps = steps - NLON * jnp.floor(steps * (1.0 / NLON))
    y = (jnp.abs(steps * (1.0 / NLON) - 0.5) - 0.25) * (2.0 * math.pi)
    z = y * y
    p = -1.0 / 39916800.0
    for c in (1.0 / 362880.0, -1.0 / 5040.0, 1.0 / 120.0, -1.0 / 6.0, 1.0):
        p = p * z + c
    return y * p


def table_rows(m_ref, table, pair):
    row = iota((8, BLK), 0)
    point = iota((8, BLK), 1).astype(F32)
    first, second, turns = [], [], []
    for u in range(2):
        base = (pair * 2 + u) * S
        orders = []
        for start, count in CHUNKS:
            tile = jnp.zeros((8, BLK), F32)
            for i in range(8):
                value = m_ref[base + start + i % count].astype(F32)
                tile = jnp.where(row == i, value, tile)
            orders.append(tile)
        turn = [2.0 * cosine(o * float(BLK)) for o in orders]
        shift = jnp.where(row >= 4, NLON // 4, 0).astype(F32)
        for c, s in ((0, 0.0), (1, 0.0), (0, NLON / 4), (1, NLON / 4), (2, shift)):
            factor = jnp.where(orders[c] == 0.0, 1.0, 2.0)
            first.append(factor * cosine(orders[c] * point + s))
            second.append(factor * cosine(orders[c] * (point + float(BLK)) + s))
            turns.append(turn[c])
    old = jnp.concatenate(first, axis=0)
    new = jnp.concatenate(second, axis=0)
    turn = jnp.concatenate(turns, axis=0)
    place = pl.ds(pl.multiple_of(pair * 2 * PR, 16), 2 * PR)
    for x in range(XB):
        table[place, x * BLK : (x + 1) * BLK] = old.astype(BF)
        old, new = new, turn * new - old


def build_table(m_ref, table, nb):
    def pair(b, _):
        table_rows(m_ref, table, b)
        return 0

    lax.fori_loop(0, nb // 2, pair, 0)


def build_spread(idx, wgt, spread, first, last):
    cells = iota((HALF, BLK), 0).astype(BF)
    zero = jnp.zeros((HALF, BLK), BF)

    def block(b, _):
        index = idx[b]
        weight = wgt[b].astype(BF)
        for h in range(2):
            spot = (index - h * HALF).astype(F32).astype(BF)
            total = None
            for t in range(TAPS):
                hit = cells == jnp.broadcast_to(spot[t : t + 1, :], (HALF, BLK))
                part = jnp.where(hit, jnp.broadcast_to(weight[t : t + 1, :], (HALF, BLK)), zero)
                total = part if total is None else total + part
            spread[b, h * HALF : (h + 1) * HALF, :] = total
        return 0

    lax.fori_loop(first, last, block, 0)


def exchange_kernel(
    nb, nl, lat, lev_dev, early, *refs
):
    (temp_ref, surf_ref, leg_ref, ord_ref, h_ref, c_ref, idx_ref, wgt_ref), refs = refs[:8], refs[8:]
    out_ref, spread = refs[:2]
    table = refs[2] if early else None
    refs = refs[2 + early :]
    (buf, leg, h, coup, idx, wgt, m_ref, rows, gall, wide, total, pieces) = refs[:12]
    (sl, sm, sa, ra, sb, rb) = refs[12:]
    band = lax.axis_index("band")
    lev = lax.axis_index("lev")
    loads = S // LOAD

    def load_temp(d):
        part = pl.ds(d * LOAD, LOAD)
        return pltpu.make_async_copy(temp_ref.at[part], buf.at[part, pl.ds(0, lev_dev)], sl.at[d])

    def load_leg(d):
        part = pl.ds(d * LOAD, LOAD)
        return pltpu.make_async_copy(leg_ref.at[part], leg.at[part], sl.at[loads + d])

    load_surf = pltpu.make_async_copy(surf_ref, buf.at[:, lev_dev], sm.at[0])
    load_h = pltpu.make_async_copy(h_ref, h, sm.at[1])
    load_c = pltpu.make_async_copy(c_ref, coup, sm.at[2])
    load_idx = pltpu.make_async_copy(idx_ref, idx, sm.at[3])
    load_wgt = pltpu.make_async_copy(wgt_ref, wgt, sm.at[4])
    load_m = pltpu.make_async_copy(ord_ref, m_ref, sm.at[5])
    load_m.start()
    load_h.start()
    load_c.start()
    load_surf.start()
    for d in range(loads):
        load_leg(d).start()
        load_temp(d).start()
    load_idx.start()
    load_wgt.start()

    barrier = pltpu.get_barrier_semaphore()

    def greet_lev(i, _):
        pl.semaphore_signal(
            barrier, inc=1, device_id=(band, lax.rem(lev + i, nl)), device_id_type=MESH
        )
        return 0

    def greet_band(i, _):
        pl.semaphore_signal(
            barrier, inc=1, device_id=(lax.rem(band + i, nb), lev), device_id_type=MESH
        )
        return 0

    lax.fori_loop(1, nl, greet_lev, 0)
    lax.fori_loop(1, nb, greet_band, 0)

    depth = nl * BLK
    lev_total = h_ref.shape[1]
    load_h.wait()
    load_c.wait()
    row = iota((lev_dev, lev_total), 0) + lev * lev_dev
    col = iota((lev_dev, lev_total), 1)
    upper = jnp.where(col >= row, h[...].astype(F32), 0.0).astype(BF)
    row = iota((depth, lev_total), 0)
    col = iota((depth, lev_total), 1)
    spots = jnp.zeros((depth, lev_total), F32)
    for v in range(nl):
        place = row - v * BLK - 2 * (col - v * lev_dev)
        inside = (col >= v * lev_dev) & (col < (v + 1) * lev_dev)
        spots = jnp.where(inside & (place >= 0) & (place < 2), 1.0, spots)
    tall = lax.dot_general(
        spots.astype(BF), upper, (((1,), (1,)), ((), ())), preferred_element_type=F32
    )
    row = iota((depth, lev_dev), 0)
    high = coup[...].astype(BF).astype(F32)
    low = coup[...] - high
    mine = lev * BLK + 2 * lev_dev
    other = lax.rem(lev + 1, nl) * BLK + 2 * lev_dev
    tall = jnp.where(
        (row == mine) | (row == mine + 1), jnp.broadcast_to(high, (depth, lev_dev)), tall
    )
    tall = jnp.where(
        (row == other) | (row == other + 1), jnp.broadcast_to(low, (depth, lev_dev)), tall
    )
    tall = tall.astype(BF)
    row = iota((lev_dev, 2 * BLK), 0)
    col = iota((lev_dev, 2 * BLK), 1)
    odd = iota((depth, 2 * BLK), 0) & 1
    right = (iota((depth, 2 * BLK), 1) >= BLK).astype(jnp.int32)
    for t in range(3):
        place = jnp.where((col & (BLK - 1)) == row + t * KP, 1.0, 0.0).astype(BF)
        full = jnp.dot(tall, place, preferred_element_type=F32)
        wide[t] = jnp.where(odd == right, full, 0.0).astype(BF)

    def copy_a(i, c):
        start, count = CHUNKS[c]
        part = pl.ds(start * lat, count * lat)
        return pltpu.make_async_remote_copy(
            src_ref=gall.at[lev, part],
            dst_ref=gall.at[lev, part],
            send_sem=sa.at[c * nl + i],
            recv_sem=ra.at[c * nl + i],
            device_id=(band, lax.rem(lev + i, nl)),
            device_id_type=MESH,
        )

    width = leg_ref.shape[2]
    order = iota((lat, width), 1)
    blank = jnp.zeros((lat, BLK - 2 * lev_dev - 2), F32)
    load_m.wait()
    load_surf.wait()
    for c, (start, count) in enumerate(CHUNKS):
        for d in range(start // LOAD, (start + count) // LOAD):
            load_leg(d).wait()
            load_temp(d).wait()
            for u in range(LOAD):
                s = d * LOAD + u
                m = m_ref[band * S + s]
                keep = jnp.where(order >= m, 1.0, 0.0).astype(BF)
                values = leg[s] * keep
                coef = buf[s].reshape(2 * lev_dev + 2, width)
                four = lax.dot_general(
                    values, coef, (((1,), (1,)), ((), ())), preferred_element_type=F32
                )
                four = jnp.concatenate([four, blank], axis=1)
                rows[pl.ds(s - start, lat, stride=count), :] = four
        gall[lev, start * lat : (start + count) * lat, :] = rows[: count * lat, :].astype(BF)
        if c == 0:
            pl.semaphore_wait(barrier, nl - 1 + nb - 1)
        for i in range(1, nl):
            copy_a(i, c).start()

    load_idx.wait()
    load_wgt.wait()
    blocks = idx.shape[0]
    build_spread(idx, wgt, spread, 0, blocks - LATE)

    for c in range(len(CHUNKS)):
        for i in range(1, nl):
            copy_a(i, c).wait()

    group = 16
    total[...] = jnp.zeros_like(total)

    def hydro(g, _):
        parts = []
        for start, count in CHUNKS:
            size = count * group
            parts.append((pl.ds(pl.multiple_of(start * lat + g * size, 16), size), size))
        left = jnp.concatenate(
            [jnp.concatenate([gall[v, p] for v in range(nl)], axis=1) for p, _ in parts], axis=0
        )
        for t in range(3):
            full = jnp.dot(left, wide[t], preferred_element_type=F32)
            for p in range(group // 2):
                at = 0
                mine = []
                for start, count in CHUNKS:
                    mine.append(full[at + p * 2 * count : at + (p + 1) * 2 * count])
                    at += count * group
                place = g * (group // 2) + p + 2 - t
                total[place] = total[place] + jnp.concatenate(mine, axis=0)
        return 0

    lax.fori_loop(0, lat // group, hydro, 0)

    def pack(b, _):
        value = total[b + 1]
        value = jnp.concatenate([value[:, :BLK], value[:, BLK:]], axis=0)
        pieces[b] = value.astype(BF)
        return 0

    lax.fori_loop(0, nb, pack, 0)

    def copy_b(i):
        peer = lax.rem(band + i, nb)
        return pltpu.make_async_remote_copy(
            src_ref=pieces.at[peer],
            dst_ref=out_ref.at[band],
            send_sem=sb.at[i],
            recv_sem=rb.at[i],
            device_id=(peer, lev),
            device_id_type=MESH,
        )

    def send(i, _):
        copy_b(i).start()
        return 0

    lax.fori_loop(1, nb, send, 0)
    out_ref[band] = pieces[band]
    build_spread(idx, wgt, spread, blocks - LATE, blocks)
    if early:
        build_table(m_ref, table, nb)

    def done(i, _):
        copy_b(i).wait()
        return 0

    lax.fori_loop(1, nb, done, 0)


def exchange(temp, surf, legendre, m_order, hydro, coupling, idx, wgt, nb, nl, early):
    _, lev_dev, _, width = temp.shape
    lat = legendre.shape[1]
    blocks = idx.shape[0]
    vmem = pl.BlockSpec(memory_space=pltpu.VMEM)
    hbm = pl.BlockSpec(memory_space=pltpu.HBM)
    out_shape = [
        jax.ShapeDtypeStruct((nb, 2 * PR, BLK), BF),
        jax.ShapeDtypeStruct((blocks, 2 * HALF, BLK), BF),
    ]
    if early:
        out_shape.append(jax.ShapeDtypeStruct((nb * PR, NLON), BF))
    return pl.pallas_call(
        functools.partial(exchange_kernel, nb, nl, lat, lev_dev, early),
        out_shape=out_shape,
        in_specs=[hbm] * 8,
        out_specs=[vmem] * len(out_shape),
        scratch_shapes=[
            pltpu.VMEM((S, lev_dev + 1, 2, width), BF),
            pltpu.VMEM(legendre.shape, BF),
            pltpu.VMEM(hydro.shape, BF),
            pltpu.VMEM(coupling.shape, F32),
            pltpu.VMEM(idx.shape, jnp.int32),
            pltpu.VMEM(wgt.shape, F32),
            pltpu.SMEM(m_order.shape, jnp.int32),
            pltpu.VMEM((8 * lat, BLK), F32),
            pltpu.VMEM((nl, S * lat, BLK), BF),
            pltpu.VMEM((3, nl * BLK, 2 * BLK), BF),
            pltpu.VMEM((nb + 2, PR, 2 * BLK), F32),
            pltpu.VMEM((nb, 2 * PR, BLK), BF),
            pltpu.SemaphoreType.DMA((2 * (S // LOAD),)),
            pltpu.SemaphoreType.DMA((6,)),
            pltpu.SemaphoreType.DMA((len(CHUNKS) * nl,)),
            pltpu.SemaphoreType.DMA((len(CHUNKS) * nl,)),
            pltpu.SemaphoreType.DMA((nb,)),
            pltpu.SemaphoreType.DMA((nb,)),
        ],
        compiler_params=pltpu.CompilerParams(
            collective_id=0, has_side_effects=True, vmem_limit_bytes=(30 if early else 52) * 1024 * 1024
        ),
    )(*[
        pltpu.with_memory_space_constraint(x, pltpu.HBM)
        for x in (temp, surf, legendre, m_order, hydro, coupling, idx, wgt)
    ])


def grid_kernel(nb, lev_dev, early, src_ref, m_ref, coef_ref, spread, *refs):
    if early:
        table, out_ref, pool = refs
    else:
        out_ref, pool, table = refs
        build_table(m_ref, table, nb)
    coef = coef_ref[...].astype(F32)
    left = []
    for p in range(2):
        tiles = []
        for b in range(nb):
            value = coef[b]
            for r in range(2):
                for c in range(2):
                    at = r * PR + c * 16 + p * 8
                    tiles.append(value[at : at + 8])
            for r in range(2):
                at = r * PR + 32 + p * 4
                tiles.append(value[at : at + 4])
        left.append(jnp.concatenate(tiles, axis=0).T)
    left = jnp.concatenate(left, axis=0).astype(BF)
    group = 4

    def synth(c, _):
        cols = pl.ds(pl.multiple_of(c * (group * BLK), 128), group * BLK)
        grid = jnp.dot(left, table[:, cols], preferred_element_type=F32).astype(BF)
        for t in range(3):
            for p in range(2):
                at = p * BLK + t * KP
                for g in range(group):
                    pool[(2 * t + p) * XB + c * group + g] = grid[
                        at : at + KP, g * BLK : (g + 1) * BLK
                    ]
        return 0

    lax.fori_loop(0, XB // group, synth, 0)

    first = (lax.axis_index("band") - 1) * (2 * XB)

    def read(b):
        source = jnp.concatenate([pool[src_ref[i, b] - first] for i in range(4)], axis=1)
        return jnp.dot(source, spread[b], preferred_element_type=F32)

    for j in range(2):

        def step(x, _):
            for u in range(8):
                xb = x * 8 + u
                out_ref[:, j, pl.ds(pl.multiple_of(xb * BLK, 128), BLK)] = read(j * XB + xb)[
                    :lev_dev
                ]
            return 0

        lax.fori_loop(0, XB // 8, step, 0)


def grid_part(src, m_order, coef, spread, table, nb, lev_dev):
    vmem = pl.BlockSpec(memory_space=pltpu.VMEM)
    smem = pl.BlockSpec(memory_space=pltpu.SMEM)
    early = len(table) > 0
    scratch = [pltpu.VMEM((JJ * XB, KP, BLK), BF)]
    if not early:
        scratch.append(pltpu.VMEM((nb * PR, NLON), BF))
    return pl.pallas_call(
        functools.partial(grid_kernel, nb, lev_dev, early),
        out_shape=jax.ShapeDtypeStruct((lev_dev, 2, NLON), F32),
        in_specs=[smem, smem] + [vmem] * (2 + len(table)),
        out_specs=vmem,
        scratch_shapes=scratch,
        compiler_params=pltpu.CompilerParams(
            vmem_limit_bytes=(24 if early else 52) * 1024 * 1024
        ),
    )(src, m_order, coef, spread, *table)


def shards(
    temp_spectrum,
    surf_spectrum,
    legendre,
    m_order,
    hydro_matrix,
    surf_coupling,
    src_blocks,
    tap_index,
    tap_weight,
):
    lev_dev = temp_spectrum.shape[3]
    nb, nl = lax.axis_size("band"), lax.axis_size("lev")
    early = nb <= 16
    coef, spread, *table = exchange(
        jnp.transpose(temp_spectrum, (0, 3, 2, 1)),
        jnp.transpose(surf_spectrum, (0, 2, 1)),
        legendre,
        m_order,
        hydro_matrix,
        surf_coupling[None, :],
        tap_index,
        tap_weight,
        nb,
        nl,
        early,
    )
    out = grid_part(src_blocks.T, m_order, coef, spread, table, nb, lev_dev)
    return jnp.transpose(out, (1, 0, 2))


def solution(mesh):
    in_specs = (
        P("band", None, None, "lev"),
        P("band", None, None),
        P("band", None, None),
        P(),
        P("lev", None),
        P("lev"),
        P("band", None),
        P("band", None, None),
        P("band", None, None),
    )
    out_specs = P("band", "lev", None)
    return jax.shard_map(shards, mesh=mesh, in_specs=in_specs, out_specs=out_specs, check_vma=False)
```

time: 45 us -> 25.9 us (0.58)
  local copies, waits for them, and re-layouts: 6.59 us -> 0.01 us
  matrix products: 5.69 us -> 0 us
  Pallas kernels: 30.3 us -> 25.7 us
  other arithmetic: 2.04 us -> 0 us
    dot_general x2 -> x0, matrix products: 5.69 us -> none  [the longest x1 4.15 us: shards(): jnp.einsum('sjn,snrk->sjrk', values, temp_spectrum, preferred_element_typ...]
    pallas_call x2, Pallas kernels: 30.3 us -> 25.7 us  [the longest x1 17.7 us: exchange(): pl.pallas_call(functools.partial(exchange_kernel, nb, nl, lat, lev_dev, e...]
    unnamed x9 -> x4, local copies, waits for them, and re-layouts: 2.12 us -> 0.01 us
    reshape x3 -> x0, local copies, waits for them, and re-layouts: 1.87 us -> none  [the longest x1 1.04 us: shards(): four = four.reshape(LR, lat_all * RS)]
    transpose x1 -> x0, other arithmetic: 1.11 us -> none  [shards(): four = jnp.transpose(four, (3, 1, 2, 0))]
    broadcast_in_dim x1 -> x0, local copies, waits for them, and re-layouts: 0.98 us -> none  [shards(): four = jnp.concatenate([four_t, four_p[..., None]], axis=3)]
    dynamic_slice x1 -> x0, local copies, waits for them, and re-layouts: 0.9 us -> none  [shards(): my_orders = lax.dynamic_slice_in_dim(m_order, band * slots, slots)]
    convert_element_type x1 -> x0, other arithmetic: 0.84 us -> none  [waves(): orders = m_order.astype(jnp.float32).reshape(nb, slots)]
where the time goes in v1:
time: 25.9 us; the launch traced here: 25.7 us
  Pallas kernels  25.7 us (99%)
    pallas_call x1, Pallas kernels, exchange(): pl.pallas_call(functools.partial(exchange_kernel, nb, nl, lat, lev_dev, e...  17.7 us
    pallas_call x1, Pallas kernels, grid_part(): pl.pallas_call(functools.partial(grid_kernel, nb, lev_dev, early), out_sh...  8.01 us

profile of v1, /device:TPU:0, one launch (start us, length us, event | category | flops | bytes accessed | tf_op | source)
XLA Modules:
  0.0 25.7 jit_solution(14480111377882656973)
XLA Ops:
  0.0 0.0 copy-start
  0.0 0.0 copy-start.1
  0.0 17.7 %shard_map.91 = (bf16[8,80,128]{2,1,0:T(8,128)(2,1)S(1)}, bf16[80,512,128]{2,1,0:T(8,128)(2,1)S(1)}, bf16[320,5120]{1,0:T(8,128)(2,1)S(1)}) custom-call(bf16[20,34,2,1280]{3,2,1,0:T(2,128)(2,1)} %bitcast.6, bf16[20,2,1280]{2,1,0:T(2,128)(2,1)} %bitcast.7, bf16[20,16,1280]{2,1,0:T(8,128)(2,1)} %refs_2_.1, s32[160]{0:T(256)} %m_ref.1, ...), custom_call_target="tpu_custom_call" | custom-call | tf_op jit(solution)/shard_map/pallas_call | solution.py:311
  17.7 0.0 copy-done
  17.7 0.0 copy-done.1
  17.7 8.0 %shard_map.92 = f32[34,2,5120]{2,1,0:T(2,128)} custom-call(s32[4,80]{1,0:T(4,128)S(1)} %bitcast.5, s32[160]{0:T(256)S(1)} %copy-done, bf16[8,80,128]{2,1,0:T(8,128)(2,1)S(1)} %get-tuple-element.8.coef_ref, bf16[80,512,128]{2,1,0:T(8,128)(2,1)S(1)} %get-tuple-element.9.spread, bf16[320,5120]{1,0:T(8,128)(2,1)S(1)} %get-tuple-element.10.refs_0_), custom_call_target="tpu_custom_call" | custom-call | tf_op jit(solution)/shard_map/pallas_call | solution.py:408
Async XLA Ops:
  0.0 17.7 %copy-start = (s32[160]{0:T(256)S(1)}, s32[160]{0:T(256)}, u32[]{:S(2)}) copy-start(s32[160]{0:T(256)} %m_ref.1) | copy-start | bytes 1924
  0.0 17.7 %copy-start.1 = (s32[80,4]{0,1:T(4,128)S(1)}, s32[80,4]{0,1:T(4,128)}, u32[]{:S(2)}) copy-start(s32[80,4]{0,1:T(4,128)} %param.15) | copy-start | bytes 3844

commit v2 on v1

--- a/solution.py
+++ b/solution.py
@@ -14,12 +14,12 @@
 XB = NLON // BLK
 S = 20
 CHUNKS = ((0, 8), (8, 8), (16, 4))
-LOAD = 4
 KP = 40
 PR = 40
 JJ = 6
 HALF = 256
-LATE = 58
+LATE = 46
+STEP = 5
 MESH = pl.DeviceIdType.MESH
 BF = jnp.bfloat16
 F32 = jnp.float32
@@ -107,15 +107,15 @@
     (sl, sm, sa, ra, sb, rb) = refs[12:]
     band = lax.axis_index("band")
     lev = lax.axis_index("lev")
-    loads = S // LOAD
-
-    def load_temp(d):
-        part = pl.ds(d * LOAD, LOAD)
-        return pltpu.make_async_copy(temp_ref.at[part], buf.at[part, pl.ds(0, lev_dev)], sl.at[d])
-
-    def load_leg(d):
-        part = pl.ds(d * LOAD, LOAD)
-        return pltpu.make_async_copy(leg_ref.at[part], leg.at[part], sl.at[loads + d])
+    chunks = len(CHUNKS)
+
+    def load_temp(c):
+        part = pl.ds(*CHUNKS[c])
+        return pltpu.make_async_copy(temp_ref.at[part], buf.at[part, pl.ds(0, lev_dev)], sl.at[c])
+
+    def load_leg(c):
+        part = pl.ds(*CHUNKS[c])
+        return pltpu.make_async_copy(leg_ref.at[part], leg.at[part], sl.at[chunks + c])
 
     load_surf = pltpu.make_async_copy(surf_ref, buf.at[:, lev_dev], sm.at[0])
     load_h = pltpu.make_async_copy(h_ref, h, sm.at[1])
@@ -124,14 +124,9 @@
     load_wgt = pltpu.make_async_copy(wgt_ref, wgt, sm.at[4])
     load_m = pltpu.make_async_copy(ord_ref, m_ref, sm.at[5])
     load_m.start()
-    load_h.start()
-    load_c.start()
     load_surf.start()
-    for d in range(loads):
-        load_leg(d).start()
-        load_temp(d).start()
-    load_idx.start()
-    load_wgt.start()
+    load_leg(0).start()
+    load_temp(0).start()
 
     barrier = pltpu.get_barrier_semaphore()
 
@@ -147,8 +142,53 @@
         )
         return 0
 
+    lax.fori_loop(1, nb, greet_band, 0)
     lax.fori_loop(1, nl, greet_lev, 0)
-    lax.fori_loop(1, nb, greet_band, 0)
+    for c in range(1, chunks):
+        load_leg(c).start()
+        load_temp(c).start()
+    load_h.start()
+    load_c.start()
+    load_idx.start()
+    load_wgt.start()
+
+    def copy_a(i, c):
+        start, count = CHUNKS[c]
+        part = pl.ds(start * lat, count * lat)
+        return pltpu.make_async_remote_copy(
+            src_ref=gall.at[lev, part],
+            dst_ref=gall.at[lev, part],
+            send_sem=sa.at[c * nl + i],
+            recv_sem=ra.at[c * nl + i],
+            device_id=(band, lax.rem(lev + i, nl)),
+            device_id_type=MESH,
+        )
+
+    width = leg_ref.shape[2]
+    order = iota((lat, width), 1)
+    blank = jnp.zeros((lat, BLK - 2 * lev_dev - 2), F32)
+    load_m.wait()
+    load_surf.wait()
+    for c, (start, count) in enumerate(CHUNKS):
+        load_leg(c).wait()
+        load_temp(c).wait()
+        for s in range(start, start + count):
+            m = m_ref[band * S + s]
+            keep = jnp.where(order >= m, 1.0, 0.0).astype(BF)
+            values = leg[s] * keep
+            coef = buf[s].reshape(2 * lev_dev + 2, width)
+            four = lax.dot_general(
+                values, coef, (((1,), (1,)), ((), ())), preferred_element_type=F32
+            )
+            four = jnp.concatenate([four, blank], axis=1)
+            rows[pl.ds(s - start, lat, stride=count), :] = four
+        gall[lev, start * lat : (start + count) * lat, :] = rows[: count * lat, :].astype(BF)
+        if c == 1:
+            pl.semaphore_wait(barrier, nl - 1 + nb - 1)
+        if c >= 1:
+            for d in range(c - 1 if c == 1 else c, c + 1):
+                for i in range(1, nl):
+                    copy_a(i, d).start()
 
     depth = nl * BLK
     lev_total = h_ref.shape[1]
@@ -188,44 +228,6 @@
         full = jnp.dot(tall, place, preferred_element_type=F32)
         wide[t] = jnp.where(odd == right, full, 0.0).astype(BF)
 
-    def copy_a(i, c):
-        start, count = CHUNKS[c]
-        part = pl.ds(start * lat, count * lat)
-        return pltpu.make_async_remote_copy(
-            src_ref=gall.at[lev, part],
-            dst_ref=gall.at[lev, part],
-            send_sem=sa.at[c * nl + i],
-            recv_sem=ra.at[c * nl + i],
-            device_id=(band, lax.rem(lev + i, nl)),
-            device_id_type=MESH,
-        )
-
-    width = leg_ref.shape[2]
-    order = iota((lat, width), 1)
-    blank = jnp.zeros((lat, BLK - 2 * lev_dev - 2), F32)
-    load_m.wait()
-    load_surf.wait()
-    for c, (start, count) in enumerate(CHUNKS):
-        for d in range(start // LOAD, (start + count) // LOAD):
-            load_leg(d).wait()
-            load_temp(d).wait()
-            for u in range(LOAD):
-                s = d * LOAD + u
-                m = m_ref[band * S + s]
-                keep = jnp.where(order >= m, 1.0, 0.0).astype(BF)
-                values = leg[s] * keep
-                coef = buf[s].reshape(2 * lev_dev + 2, width)
-                four = lax.dot_general(
-                    values, coef, (((1,), (1,)), ((), ())), preferred_element_type=F32
-                )
-                four = jnp.concatenate([four, blank], axis=1)
-                rows[pl.ds(s - start, lat, stride=count), :] = four
-        gall[lev, start * lat : (start + count) * lat, :] = rows[: count * lat, :].astype(BF)
-        if c == 0:
-            pl.semaphore_wait(barrier, nl - 1 + nb - 1)
-        for i in range(1, nl):
-            copy_a(i, c).start()
-
     load_idx.wait()
     load_wgt.wait()
     blocks = idx.shape[0]
@@ -236,37 +238,60 @@
             copy_a(i, c).wait()
 
     group = 16
-    total[...] = jnp.zeros_like(total)
-
-    def hydro(g, _):
+    pairs = group // 2
+
+    def hydro(g):
         parts = []
         for start, count in CHUNKS:
             size = count * group
-            parts.append((pl.ds(pl.multiple_of(start * lat + g * size, 16), size), size))
+            at = start * lat + g * size
+            parts.append((pl.ds(at if isinstance(at, int) else pl.multiple_of(at, 16), size), size))
         left = jnp.concatenate(
             [jnp.concatenate([gall[v, p] for v in range(nl)], axis=1) for p, _ in parts], axis=0
         )
+        result = []
         for t in range(3):
             full = jnp.dot(left, wide[t], preferred_element_type=F32)
-            for p in range(group // 2):
+            split = []
+            for p in range(pairs):
                 at = 0
                 mine = []
                 for start, count in CHUNKS:
                     mine.append(full[at + p * 2 * count : at + (p + 1) * 2 * count])
                     at += count * group
-                place = g * (group // 2) + p + 2 - t
-                total[place] = total[place] + jnp.concatenate(mine, axis=0)
-        return 0
-
-    lax.fori_loop(0, lat // group, hydro, 0)
-
-    def pack(b, _):
-        value = total[b + 1]
+                split.append(jnp.concatenate(mine, axis=0))
+            result.append(split)
+        return result
+
+    def pack(b, value):
         value = jnp.concatenate([value[:, :BLK], value[:, BLK:]], axis=0)
         pieces[b] = value.astype(BF)
-        return 0
-
-    lax.fori_loop(0, nb, pack, 0)
+
+    if lat == group:
+        result = hydro(0)
+        for b in range(nb):
+            value = result[1][b]
+            for t in (0, 2):
+                if 0 <= b - 1 + t < pairs:
+                    value = value + result[t][b - 1 + t]
+            pack(b, value)
+    else:
+        total[...] = jnp.zeros_like(total)
+
+        def many(g, _):
+            result = hydro(g)
+            for t in range(3):
+                for p in range(pairs):
+                    place = g * pairs + p + 2 - t
+                    total[place] = total[place] + result[t][p]
+            return 0
+
+        def finish(b, _):
+            pack(b, total[b + 1])
+            return 0
+
+        lax.fori_loop(0, lat // group, many, 0)
+        lax.fori_loop(0, nb, finish, 0)
 
     def copy_b(i):
         peer = lax.rem(band + i, nb)
@@ -324,9 +349,9 @@
             pltpu.VMEM((8 * lat, BLK), F32),
             pltpu.VMEM((nl, S * lat, BLK), BF),
             pltpu.VMEM((3, nl * BLK, 2 * BLK), BF),
-            pltpu.VMEM((nb + 2, PR, 2 * BLK), F32),
+            pltpu.VMEM((nb + 2 if lat > 16 else 1, PR, 2 * BLK), F32),
             pltpu.VMEM((nb, 2 * PR, BLK), BF),
-            pltpu.SemaphoreType.DMA((2 * (S // LOAD),)),
+            pltpu.SemaphoreType.DMA((2 * len(CHUNKS),)),
             pltpu.SemaphoreType.DMA((6,)),
             pltpu.SemaphoreType.DMA((len(CHUNKS) * nl,)),
             pltpu.SemaphoreType.DMA((len(CHUNKS) * nl,)),
@@ -342,12 +367,14 @@
     ])
 
 
-def grid_kernel(nb, lev_dev, early, src_ref, m_ref, coef_ref, spread, *refs):
+def grid_kernel(nb, lev_dev, early, src_ref, coef_ref, spread, *refs):
     if early:
-        table, out_ref, pool = refs
+        table, out_ref, src, pool, grid, ss, so = refs
     else:
-        out_ref, pool, table = refs
+        m_ref, out_ref, src, pool, grid, ss, so, table = refs
         build_table(m_ref, table, nb)
+    load_src = pltpu.make_async_copy(src_ref, src, ss)
+    load_src.start()
     coef = coef_ref[...].astype(F32)
     left = []
     for p in range(2):
@@ -367,54 +394,65 @@
 
     def synth(c, _):
         cols = pl.ds(pl.multiple_of(c * (group * BLK), 128), group * BLK)
-        grid = jnp.dot(left, table[:, cols], preferred_element_type=F32).astype(BF)
+        value = jnp.dot(left, table[:, cols], preferred_element_type=F32).astype(BF)
         for t in range(3):
             for p in range(2):
                 at = p * BLK + t * KP
                 for g in range(group):
-                    pool[(2 * t + p) * XB + c * group + g] = grid[
+                    pool[(2 * t + p) * XB + c * group + g] = value[
                         at : at + KP, g * BLK : (g + 1) * BLK
                     ]
         return 0
 
-    lax.fori_loop(0, XB // group, synth, 0)
+    lax.fori_loop(0, XB // group, synth, 0, unroll=XB // group if early else 1)
+    load_src.wait()
 
     first = (lax.axis_index("band") - 1) * (2 * XB)
 
     def read(b):
-        source = jnp.concatenate([pool[src_ref[i, b] - first] for i in range(4)], axis=1)
+        source = jnp.concatenate([pool[src[i, b] - first] for i in range(4)], axis=1)
         return jnp.dot(source, spread[b], preferred_element_type=F32)
 
-    for j in range(2):
-
-        def step(x, _):
-            for u in range(8):
-                xb = x * 8 + u
-                out_ref[:, j, pl.ds(pl.multiple_of(xb * BLK, 128), BLK)] = read(j * XB + xb)[
-                    :lev_dev
-                ]
-            return 0
-
-        lax.fori_loop(0, XB // 8, step, 0)
+    def write(q):
+        cols = pl.ds(q * (STEP * BLK), STEP * BLK)
+        return pltpu.make_async_copy(grid.at[:, :, cols], out_ref.at[:, :, cols], so.at[q])
+
+    for q in range(XB // STEP):
+        for x in range(q * STEP, (q + 1) * STEP):
+            for j in range(2):
+                grid[:, j, x * BLK : (x + 1) * BLK] = read(j * XB + x)[:lev_dev]
+        write(q).start()
+    for q in range(XB // STEP):
+        write(q).wait()
 
 
 def grid_part(src, m_order, coef, spread, table, nb, lev_dev):
     vmem = pl.BlockSpec(memory_space=pltpu.VMEM)
-    smem = pl.BlockSpec(memory_space=pltpu.SMEM)
+    hbm = pl.BlockSpec(memory_space=pltpu.HBM)
     early = len(table) > 0
-    scratch = [pltpu.VMEM((JJ * XB, KP, BLK), BF)]
-    if not early:
+    scratch = [
+        pltpu.SMEM(src.shape, jnp.int32),
+        pltpu.VMEM((JJ * XB, KP, BLK), BF),
+        pltpu.VMEM((lev_dev, 2, NLON), F32),
+        pltpu.SemaphoreType.DMA,
+        pltpu.SemaphoreType.DMA((XB // STEP,)),
+    ]
+    src = pltpu.with_memory_space_constraint(src, pltpu.HBM)
+    if early:
+        last, specs = list(table), [vmem]
+    else:
+        last, specs = [m_order], [pl.BlockSpec(memory_space=pltpu.SMEM)]
         scratch.append(pltpu.VMEM((nb * PR, NLON), BF))
     return pl.pallas_call(
         functools.partial(grid_kernel, nb, lev_dev, early),
         out_shape=jax.ShapeDtypeStruct((lev_dev, 2, NLON), F32),
-        in_specs=[smem, smem] + [vmem] * (2 + len(table)),
-        out_specs=vmem,
+        in_specs=[hbm, vmem, vmem] + specs,
+        out_specs=hbm,
         scratch_shapes=scratch,
         compiler_params=pltpu.CompilerParams(
-            vmem_limit_bytes=(24 if early else 52) * 1024 * 1024
+            vmem_limit_bytes=(24 if early else 54) * 1024 * 1024
         ),
-    )(src, m_order, coef, spread, *table)
+    )(src, coef, spread, *last)
 
 
 def shards(

time: 25.9 us -> 22.4 us (0.86)
  Pallas kernels: 25.7 us -> 22.2 us
    pallas_call x1, Pallas kernels: 8.01 us -> 4.9 us  [grid_part(): pl.pallas_call(functools.partial(grid_kernel, nb, lev_dev, early), out_sh...]
    pallas_call x1, Pallas kernels: 17.7 us -> 17.3 us  [exchange(): pl.pallas_call(functools.partial(exchange_kernel, nb, nl, lat, lev_dev, e...]
where the time goes in v2:
time: 22.4 us; the launch traced here: 22.2 us
  Pallas kernels  22.2 us (99%)
    pallas_call x1, Pallas kernels, exchange(): pl.pallas_call(functools.partial(exchange_kernel, nb, nl, lat, lev_dev, e...  17.3 us
    pallas_call x1, Pallas kernels, grid_part(): pl.pallas_call(functools.partial(grid_kernel, nb, lev_dev, early), out_sh...  4.9 us

profile of v2, /device:TPU:0, one launch (start us, length us, event | category | flops | bytes accessed | tf_op | source)
XLA Modules:
  0.0 22.2 jit_solution(17162965772954811267)
XLA Ops:
  0.0 17.3 %shard_map.91 = (bf16[8,80,128]{2,1,0:T(8,128)(2,1)S(1)}, bf16[80,512,128]{2,1,0:T(8,128)(2,1)S(1)}, bf16[320,5120]{1,0:T(8,128)(2,1)S(1)}) custom-call(bf16[20,34,2,1280]{3,2,1,0:T(2,128)(2,1)} %bitcast.5, bf16[20,2,1280]{2,1,0:T(2,128)(2,1)} %bitcast.6, bf16[20,16,1280]{2,1,0:T(8,128)(2,1)} %refs_2_.1, s32[160]{0:T(256)} %refs_3_.1, ...), custom_call_target="tpu_custom_call" | custom-call | tf_op jit(solution)/shard_map/pallas_call | solution.py:336
  17.3 4.9 %shard_map.92 = f32[34,2,5120]{2,1,0:T(2,128)} custom-call(s32[4,80]{1,0:T(4,128)} %bitcast.7, bf16[8,80,128]{2,1,0:T(8,128)(2,1)S(1)} %get-tuple-element.8.coef_ref, bf16[80,512,128]{2,1,0:T(8,128)(2,1)S(1)} %get-tuple-element.9.spread, bf16[320,5120]{1,0:T(8,128)(2,1)S(1)} %get-tuple-element.10.refs_0_), custom_call_target="tpu_custom_call" | custom-call | tf_op jit(solution)/shard_map/pallas_call | solution.py:446

commit v3 on v2

--- a/solution.py
+++ b/solution.py
@@ -14,6 +14,8 @@
 XB = NLON // BLK
 S = 20
 CHUNKS = ((0, 8), (8, 8), (16, 4))
+Q = 4
+BLOCKS = S // Q
 KP = 40
 PR = 40
 JJ = 6
@@ -103,8 +105,8 @@
     out_ref, spread = refs[:2]
     table = refs[2] if early else None
     refs = refs[2 + early :]
-    (buf, leg, h, coup, idx, wgt, m_ref, rows, gall, wide, total, pieces) = refs[:12]
-    (sl, sm, sa, ra, sb, rb) = refs[12:]
+    (buf, leg, h, coup, idx, wgt, m_ref, rows, gall, full, wide, total, pieces) = refs[:13]
+    (sl, sm, sa, ra, sb, rb) = refs[13:]
     band = lax.axis_index("band")
     lev = lax.axis_index("lev")
     chunks = len(CHUNKS)
@@ -153,8 +155,7 @@
     load_wgt.start()
 
     def copy_a(i, c):
-        start, count = CHUNKS[c]
-        part = pl.ds(start * lat, count * lat)
+        part = pl.ds(c * Q * lat, Q * lat)
         return pltpu.make_async_remote_copy(
             src_ref=gall.at[lev, part],
             dst_ref=gall.at[lev, part],
@@ -165,30 +166,51 @@
         )
 
     width = leg_ref.shape[2]
+    used = 2 * lev_dev
+    tail = 2 * used - BLK
+    spare = used + 4
     order = iota((lat, width), 1)
-    blank = jnp.zeros((lat, BLK - 2 * lev_dev - 2), F32)
+    lane = iota((lat, BLK), 1)
+    blank = jnp.zeros((lat, BLK - used - 2), F32)
+
+    def transform(s):
+        m = m_ref[band * S + s]
+        keep = jnp.where(order >= m, 1.0, 0.0).astype(BF)
+        coef = buf[s].reshape(used + 2, width)
+        four = lax.dot_general(
+            leg[s] * keep, coef, (((1,), (1,)), ((), ())), preferred_element_type=F32
+        )
+        return jnp.concatenate([four, blank], axis=1)
+
+    def place(block, q, value):
+        rows[block, pl.ds(q, lat, stride=Q), :] = value
+
     load_m.wait()
     load_surf.wait()
+    ends = [None] * Q
     for c, (start, count) in enumerate(CHUNKS):
         load_leg(c).wait()
         load_temp(c).wait()
-        for s in range(start, start + count):
-            m = m_ref[band * S + s]
-            keep = jnp.where(order >= m, 1.0, 0.0).astype(BF)
-            values = leg[s] * keep
-            coef = buf[s].reshape(2 * lev_dev + 2, width)
-            four = lax.dot_general(
-                values, coef, (((1,), (1,)), ((), ())), preferred_element_type=F32
-            )
-            four = jnp.concatenate([four, blank], axis=1)
-            rows[pl.ds(s - start, lat, stride=count), :] = four
-        gall[lev, start * lat : (start + count) * lat, :] = rows[: count * lat, :].astype(BF)
+        for q in range(Q):
+            one = transform(start + q)
+            place(start // Q, q, one)
+            if count == 2 * Q:
+                two = transform(start + Q + q)
+                place(start // Q + 1, q, two)
+                place(BLOCKS + c, q, jnp.where(lane < used, one, pltpu.roll(two, used, 1)))
+                end = pltpu.roll(two, spare + c * tail - used + tail, 1)
+                ends[q] = end if c == 0 else jnp.where(lane < spare + c * tail, ends[q], end)
+            else:
+                place(BLOCKS + c, q, jnp.where(lane < used, one, ends[q]))
+        gall[lev, c * Q * lat : (c + 1) * Q * lat, :] = rows[BLOCKS + c].astype(BF)
         if c == 1:
             pl.semaphore_wait(barrier, nl - 1 + nb - 1)
         if c >= 1:
             for d in range(c - 1 if c == 1 else c, c + 1):
                 for i in range(1, nl):
                     copy_a(i, d).start()
+    for k in range(BLOCKS):
+        full[lev, k * Q * lat : (k + 1) * Q * lat, :] = rows[k].astype(BF)
 
     depth = nl * BLK
     lev_total = h_ref.shape[1]
@@ -201,22 +223,16 @@
     col = iota((depth, lev_total), 1)
     spots = jnp.zeros((depth, lev_total), F32)
     for v in range(nl):
-        place = row - v * BLK - 2 * (col - v * lev_dev)
+        step = row - v * BLK - 2 * (col - v * lev_dev)
         inside = (col >= v * lev_dev) & (col < (v + 1) * lev_dev)
-        spots = jnp.where(inside & (place >= 0) & (place < 2), 1.0, spots)
+        spots = jnp.where(inside & (step >= 0) & (step < 2), 1.0, spots)
     tall = lax.dot_general(
         spots.astype(BF), upper, (((1,), (1,)), ((), ())), preferred_element_type=F32
     )
     row = iota((depth, lev_dev), 0)
-    high = coup[...].astype(BF).astype(F32)
-    low = coup[...] - high
     mine = lev * BLK + 2 * lev_dev
-    other = lax.rem(lev + 1, nl) * BLK + 2 * lev_dev
     tall = jnp.where(
-        (row == mine) | (row == mine + 1), jnp.broadcast_to(high, (depth, lev_dev)), tall
-    )
-    tall = jnp.where(
-        (row == other) | (row == other + 1), jnp.broadcast_to(low, (depth, lev_dev)), tall
+        (row == mine) | (row == mine + 1), jnp.broadcast_to(coup[...], (depth, lev_dev)), tall
     )
     tall = tall.astype(BF)
     row = iota((lev_dev, 2 * BLK), 0)
@@ -224,9 +240,9 @@
     odd = iota((depth, 2 * BLK), 0) & 1
     right = (iota((depth, 2 * BLK), 1) >= BLK).astype(jnp.int32)
     for t in range(3):
-        place = jnp.where((col & (BLK - 1)) == row + t * KP, 1.0, 0.0).astype(BF)
-        full = jnp.dot(tall, place, preferred_element_type=F32)
-        wide[t] = jnp.where(odd == right, full, 0.0).astype(BF)
+        onto = jnp.where((col & (BLK - 1)) == row + t * KP, 1.0, 0.0).astype(BF)
+        spread_out = jnp.dot(tall, onto, preferred_element_type=F32)
+        wide[t] = jnp.where(odd == right, spread_out, 0.0).astype(BF)
 
     load_idx.wait()
     load_wgt.wait()
@@ -236,31 +252,37 @@
     for c in range(len(CHUNKS)):
         for i in range(1, nl):
             copy_a(i, c).wait()
+    size = Q * lat
+    lane = iota((size, BLK), 1)
+    for i in range(1, nl):
+        v = lax.rem(lev + i, nl)
+        last = gall[v, 2 * size : 3 * size, :]
+        full[v, 4 * size : 5 * size, :] = last
+        last = last.astype(F32)
+        for c in range(2):
+            pair = gall[v, c * size : (c + 1) * size, :]
+            full[v, 2 * c * size : (2 * c + 1) * size, :] = pair
+            end = pltpu.roll(last, 2 * BLK + used - tail - spare - c * tail - BLK, 1)
+            pair = jnp.where(lane < used - tail, pltpu.roll(pair.astype(F32), BLK - used, 1), end)
+            full[v, (2 * c + 1) * size : (2 * c + 2) * size, :] = pair.astype(BF)
 
     group = 16
     pairs = group // 2
 
     def hydro(g):
         parts = []
-        for start, count in CHUNKS:
-            size = count * group
-            at = start * lat + g * size
-            parts.append((pl.ds(at if isinstance(at, int) else pl.multiple_of(at, 16), size), size))
+        for k in range(BLOCKS):
+            at = k * Q * lat + g * Q * group
+            at = at if isinstance(at, int) else pl.multiple_of(at, 16)
+            parts.append(pl.ds(at, Q * group))
         left = jnp.concatenate(
-            [jnp.concatenate([gall[v, p] for v in range(nl)], axis=1) for p, _ in parts], axis=0
+            [jnp.concatenate([full[v, p] for v in range(nl)], axis=1) for p in parts], axis=0
         )
         result = []
         for t in range(3):
-            full = jnp.dot(left, wide[t], preferred_element_type=F32)
-            split = []
-            for p in range(pairs):
-                at = 0
-                mine = []
-                for start, count in CHUNKS:
-                    mine.append(full[at + p * 2 * count : at + (p + 1) * 2 * count])
-                    at += count * group
-                split.append(jnp.concatenate(mine, axis=0))
-            result.append(split)
+            value = jnp.dot(left, wide[t], preferred_element_type=F32)
+            value = value.reshape(BLOCKS, pairs, 2 * Q, 2 * BLK)
+            result.append([value[:, p].reshape(PR, 2 * BLK) for p in range(pairs)])
         return result
 
     def pack(b, value):
@@ -346,7 +368,8 @@
             pltpu.VMEM(idx.shape, jnp.int32),
             pltpu.VMEM(wgt.shape, F32),
             pltpu.SMEM(m_order.shape, jnp.int32),
-            pltpu.VMEM((8 * lat, BLK), F32),
+            pltpu.VMEM((BLOCKS + len(CHUNKS), Q * lat, BLK), F32),
+            pltpu.VMEM((nl, len(CHUNKS) * Q * lat, BLK), BF),
             pltpu.VMEM((nl, S * lat, BLK), BF),
             pltpu.VMEM((3, nl * BLK, 2 * BLK), BF),
             pltpu.VMEM((nb + 2 if lat > 16 else 1, PR, 2 * BLK), F32),
@@ -381,13 +404,9 @@
         tiles = []
         for b in range(nb):
             value = coef[b]
-            for r in range(2):
-                for c in range(2):
-                    at = r * PR + c * 16 + p * 8
-                    tiles.append(value[at : at + 8])
-            for r in range(2):
-                at = r * PR + 32 + p * 4
-                tiles.append(value[at : at + 4])
+            for r, k in [(r, k) for r in range(2) for k in range(4)] + [(0, 4), (1, 4)]:
+                at = r * PR + k * 2 * Q + p * Q
+                tiles.append(value[at : at + Q])
         left.append(jnp.concatenate(tiles, axis=0).T)
     left = jnp.concatenate(left, axis=0).astype(BF)
     group = 4

time: 22.4 us -> 21 us (0.938)
  Pallas kernels: 22.2 us -> 20.8 us
    pallas_call x1, Pallas kernels: 17.3 us -> 15.9 us  [exchange(): pl.pallas_call(functools.partial(exchange_kernel, nb, nl, lat, lev_dev, e...]
where the time goes in v3:
time: 21 us; the launch traced here: 20.9 us
  Pallas kernels  20.8 us (99%)
    pallas_call x1, Pallas kernels, exchange(): pl.pallas_call(functools.partial(exchange_kernel, nb, nl, lat, lev_dev, e...  15.9 us
    pallas_call x1, Pallas kernels, grid_part(): pl.pallas_call(functools.partial(grid_kernel, nb, lev_dev, early), out_sh...  4.9 us

profile of v3, /device:TPU:0, one launch (start us, length us, event | category | flops | bytes accessed | tf_op | source)
XLA Modules:
  0.0 20.9 jit_solution(17047859251806958147)
XLA Ops:
  0.0 15.9 %shard_map.91 = (bf16[8,80,128]{2,1,0:T(8,128)(2,1)S(1)}, bf16[80,512,128]{2,1,0:T(8,128)(2,1)S(1)}, bf16[320,5120]{1,0:T(8,128)(2,1)S(1)}) custom-call(bf16[20,34,2,1280]{3,2,1,0:T(2,128)(2,1)} %bitcast.5, bf16[20,2,1280]{2,1,0:T(2,128)(2,1)} %bitcast.6, bf16[20,16,1280]{2,1,0:T(8,128)(2,1)} %refs_2_.1, s32[160]{0:T(256)} %refs_3_.1, ...), custom_call_target="tpu_custom_call" | custom-call | tf_op jit(solution)/shard_map/pallas_call | solution.py:358
  16.0 4.9 %shard_map.92 = f32[34,2,5120]{2,1,0:T(2,128)} custom-call(s32[4,80]{1,0:T(4,128)} %bitcast.7, bf16[8,80,128]{2,1,0:T(8,128)(2,1)S(1)} %get-tuple-element.8.coef_ref, bf16[80,512,128]{2,1,0:T(8,128)(2,1)S(1)} %get-tuple-element.9.spread, bf16[320,5120]{1,0:T(8,128)(2,1)S(1)} %get-tuple-element.10.refs_0_), custom_call_target="tpu_custom_call" | custom-call | tf_op jit(solution)/shard_map/pallas_call | solution.py:465

commit v4 on v3

--- a/solution.py
+++ b/solution.py
@@ -120,6 +120,7 @@
         return pltpu.make_async_copy(leg_ref.at[part], leg.at[part], sl.at[chunks + c])
 
     load_surf = pltpu.make_async_copy(surf_ref, buf.at[:, lev_dev], sm.at[0])
+    load_again = pltpu.make_async_copy(surf_ref, buf.at[:, lev_dev + 1], sm.at[6])
     load_h = pltpu.make_async_copy(h_ref, h, sm.at[1])
     load_c = pltpu.make_async_copy(c_ref, coup, sm.at[2])
     load_idx = pltpu.make_async_copy(idx_ref, idx, sm.at[3])
@@ -127,6 +128,7 @@
     load_m = pltpu.make_async_copy(ord_ref, m_ref, sm.at[5])
     load_m.start()
     load_surf.start()
+    load_again.start()
     load_leg(0).start()
     load_temp(0).start()
 
@@ -171,12 +173,12 @@
     spare = used + 4
     order = iota((lat, width), 1)
     lane = iota((lat, BLK), 1)
-    blank = jnp.zeros((lat, BLK - used - 2), F32)
+    blank = jnp.zeros((lat, BLK - used - 4), F32)
 
     def transform(s):
         m = m_ref[band * S + s]
         keep = jnp.where(order >= m, 1.0, 0.0).astype(BF)
-        coef = buf[s].reshape(used + 2, width)
+        coef = buf[s].reshape(used + 4, width)
         four = lax.dot_general(
             leg[s] * keep, coef, (((1,), (1,)), ((), ())), preferred_element_type=F32
         )
@@ -187,6 +189,7 @@
 
     load_m.wait()
     load_surf.wait()
+    load_again.wait()
     ends = [None] * Q
     for c, (start, count) in enumerate(CHUNKS):
         load_leg(c).wait()
@@ -203,12 +206,10 @@
             else:
                 place(BLOCKS + c, q, jnp.where(lane < used, one, ends[q]))
         gall[lev, c * Q * lat : (c + 1) * Q * lat, :] = rows[BLOCKS + c].astype(BF)
-        if c == 1:
+        if c == 0:
             pl.semaphore_wait(barrier, nl - 1 + nb - 1)
-        if c >= 1:
-            for d in range(c - 1 if c == 1 else c, c + 1):
-                for i in range(1, nl):
-                    copy_a(i, d).start()
+        for i in range(1, nl):
+            copy_a(i, c).start()
     for k in range(BLOCKS):
         full[lev, k * Q * lat : (k + 1) * Q * lat, :] = rows[k].astype(BF)
 
@@ -231,8 +232,14 @@
     )
     row = iota((depth, lev_dev), 0)
     mine = lev * BLK + 2 * lev_dev
+    high = coup[...].astype(BF).astype(F32)
     tall = jnp.where(
-        (row == mine) | (row == mine + 1), jnp.broadcast_to(coup[...], (depth, lev_dev)), tall
+        (row == mine) | (row == mine + 1), jnp.broadcast_to(high, (depth, lev_dev)), tall
+    )
+    tall = jnp.where(
+        (row == mine + 2) | (row == mine + 3),
+        jnp.broadcast_to(coup[...] - high, (depth, lev_dev)),
+        tall,
     )
     tall = tall.astype(BF)
     row = iota((lev_dev, 2 * BLK), 0)
@@ -361,7 +368,7 @@
         in_specs=[hbm] * 8,
         out_specs=[vmem] * len(out_shape),
         scratch_shapes=[
-            pltpu.VMEM((S, lev_dev + 1, 2, width), BF),
+            pltpu.VMEM((S, lev_dev + 2, 2, width), BF),
             pltpu.VMEM(legendre.shape, BF),
             pltpu.VMEM(hydro.shape, BF),
             pltpu.VMEM(coupling.shape, F32),
@@ -375,7 +382,7 @@
             pltpu.VMEM((nb + 2 if lat > 16 else 1, PR, 2 * BLK), F32),
             pltpu.VMEM((nb, 2 * PR, BLK), BF),
             pltpu.SemaphoreType.DMA((2 * len(CHUNKS),)),
-            pltpu.SemaphoreType.DMA((6,)),
+            pltpu.SemaphoreType.DMA((7,)),
             pltpu.SemaphoreType.DMA((len(CHUNKS) * nl,)),
             pltpu.SemaphoreType.DMA((len(CHUNKS) * nl,)),
             pltpu.SemaphoreType.DMA((nb,)),

time: 21 us -> 20.7 us (0.986)
  Pallas kernels: 20.8 us -> 20.5 us
    pallas_call x1, Pallas kernels: 15.9 us -> 15.6 us  [exchange(): pl.pallas_call(functools.partial(exchange_kernel, nb, nl, lat, lev_dev, e...]
where the time goes in v4:
time: 20.7 us; the launch traced here: 20.6 us
  Pallas kernels  20.5 us (99%)
    pallas_call x1, Pallas kernels, exchange(): pl.pallas_call(functools.partial(exchange_kernel, nb, nl, lat, lev_dev, e...  15.6 us
    pallas_call x1, Pallas kernels, grid_part(): pl.pallas_call(functools.partial(grid_kernel, nb, lev_dev, early), out_sh...  4.89 us

profile of v4, /device:TPU:0, one launch (start us, length us, event | category | flops | bytes accessed | tf_op | source)
XLA Modules:
  0.0 20.6 jit_solution(9162074544964582871)
XLA Ops:
  0.0 15.6 %shard_map.91 = (bf16[8,80,128]{2,1,0:T(8,128)(2,1)S(1)}, bf16[80,512,128]{2,1,0:T(8,128)(2,1)S(1)}, bf16[320,5120]{1,0:T(8,128)(2,1)S(1)}) custom-call(bf16[20,34,2,1280]{3,2,1,0:T(2,128)(2,1)} %bitcast.5, bf16[20,2,1280]{2,1,0:T(2,128)(2,1)} %bitcast.6, bf16[20,16,1280]{2,1,0:T(8,128)(2,1)} %refs_2_.1, s32[160]{0:T(256)} %refs_3_.1, ...), custom_call_target="tpu_custom_call" | custom-call | tf_op jit(solution)/shard_map/pallas_call | solution.py:365
  15.7 4.9 %shard_map.92 = f32[34,2,5120]{2,1,0:T(2,128)} custom-call(s32[4,80]{1,0:T(4,128)} %bitcast.7, bf16[8,80,128]{2,1,0:T(8,128)(2,1)S(1)} %get-tuple-element.8.coef_ref, bf16[80,512,128]{2,1,0:T(8,128)(2,1)S(1)} %get-tuple-element.9.spread, bf16[320,5120]{1,0:T(8,128)(2,1)S(1)} %get-tuple-element.10.refs_0_), custom_call_target="tpu_custom_call" | custom-call | tf_op jit(solution)/shard_map/pallas_call | solution.py:472

commit v5 on v4

--- a/solution.py
+++ b/solution.py
@@ -12,6 +12,8 @@
 BLK = 128
 TAPS = 4
 XB = NLON // BLK
+XH = XB // 2
+HALF_LON = NLON // 2
 S = 20
 CHUNKS = ((0, 8), (8, 8), (16, 4))
 Q = 4
@@ -20,7 +22,7 @@
 PR = 40
 JJ = 6
 HALF = 256
-LATE = 46
+WORK = (10, 40, 30, 0)
 STEP = 5
 MESH = pl.DeviceIdType.MESH
 BF = jnp.bfloat16
@@ -41,10 +43,10 @@
     return y * p
 
 
-def table_rows(m_ref, table, pair):
+def table_rows(m_ref, table, signs, pair):
     row = iota((8, BLK), 0)
     point = iota((8, BLK), 1).astype(F32)
-    first, second, turns = [], [], []
+    first, second, turns, parity = [], [], [], []
     for u in range(2):
         base = (pair * 2 + u) * S
         orders = []
@@ -61,18 +63,21 @@
             first.append(factor * cosine(orders[c] * point + s))
             second.append(factor * cosine(orders[c] * (point + float(BLK)) + s))
             turns.append(turn[c])
+            half = orders[c] * 0.5
+            parity.append(1.0 - 4.0 * (half - jnp.floor(half)))
     old = jnp.concatenate(first, axis=0)
     new = jnp.concatenate(second, axis=0)
     turn = jnp.concatenate(turns, axis=0)
     place = pl.ds(pl.multiple_of(pair * 2 * PR, 16), 2 * PR)
-    for x in range(XB):
+    signs[place, :] = jnp.concatenate(parity, axis=0)
+    for x in range(XH):
         table[place, x * BLK : (x + 1) * BLK] = old.astype(BF)
         old, new = new, turn * new - old
 
 
-def build_table(m_ref, table, nb):
+def build_table(m_ref, table, signs, nb):
     def pair(b, _):
-        table_rows(m_ref, table, b)
+        table_rows(m_ref, table, signs, b)
         return 0
 
     lax.fori_loop(0, nb // 2, pair, 0)
@@ -98,15 +103,40 @@
     lax.fori_loop(first, last, block, 0)
 
 
+def assemble(coef, sign):
+    left = []
+    for p in range(2):
+        tiles = []
+        for b in range(coef.shape[0]):
+            value = coef[b].astype(F32)
+            for r, k in [(r, k) for r in range(2) for k in range(4)] + [(0, 4), (1, 4)]:
+                at = r * PR + k * 2 * Q + p * Q
+                tiles.append(value[at : at + Q])
+        left.append(jnp.concatenate(tiles, axis=0).T)
+    left = jnp.concatenate(left, axis=0)
+    return jnp.concatenate([left, left * sign], axis=0).astype(BF)
+
+
+def halves(band, nb):
+    half = nb // 2
+    near = (band // half) * half
+    return half, near, lax.rem(near + half, nb)
+
+
+def table_part(table, start, half, cols):
+    return table[pl.ds(pl.multiple_of(start * PR, 16), half * PR), cols]
+
+
 def exchange_kernel(
     nb, nl, lat, lev_dev, early, *refs
 ):
     (temp_ref, surf_ref, leg_ref, ord_ref, h_ref, c_ref, idx_ref, wgt_ref), refs = refs[:8], refs[8:]
     out_ref, spread = refs[:2]
-    table = refs[2] if early else None
-    refs = refs[2 + early :]
-    (buf, leg, h, coup, idx, wgt, m_ref, rows, gall, full, wide, total, pieces) = refs[:13]
-    (sl, sm, sa, ra, sb, rb) = refs[13:]
+    if early:
+        table, partial, sign = refs[2:5]
+    refs = refs[2 + 3 * early :]
+    (buf, leg, h, coup, idx, wgt, m_ref, rows, gall, full, wide, total, pieces, signs) = refs[:14]
+    (sl, sm, sa, ra, sb, rb) = refs[14:]
     band = lax.axis_index("band")
     lev = lax.axis_index("lev")
     chunks = len(CHUNKS)
@@ -126,6 +156,8 @@
     load_idx = pltpu.make_async_copy(idx_ref, idx, sm.at[3])
     load_wgt = pltpu.make_async_copy(wgt_ref, wgt, sm.at[4])
     load_m = pltpu.make_async_copy(ord_ref, m_ref, sm.at[5])
+    load_idx.start()
+    load_wgt.start()
     load_m.start()
     load_surf.start()
     load_again.start()
@@ -153,8 +185,17 @@
         load_temp(c).start()
     load_h.start()
     load_c.start()
-    load_idx.start()
-    load_wgt.start()
+    load_idx.wait()
+    load_wgt.wait()
+    marks = [0]
+    for count in WORK:
+        marks.append(marks[-1] + count)
+    assert marks[-1] == idx.shape[0]
+
+    def build(part):
+        build_spread(idx, wgt, spread, marks[part], marks[part + 1])
+
+    build(0)
 
     def copy_a(i, c):
         part = pl.ds(c * Q * lat, Q * lat)
@@ -251,10 +292,7 @@
         spread_out = jnp.dot(tall, onto, preferred_element_type=F32)
         wide[t] = jnp.where(odd == right, spread_out, 0.0).astype(BF)
 
-    load_idx.wait()
-    load_wgt.wait()
-    blocks = idx.shape[0]
-    build_spread(idx, wgt, spread, 0, blocks - LATE)
+    build(1)
 
     for c in range(len(CHUNKS)):
         for i in range(1, nl):
@@ -339,15 +377,46 @@
 
     lax.fori_loop(1, nb, send, 0)
     out_ref[band] = pieces[band]
-    build_spread(idx, wgt, spread, blocks - LATE, blocks)
+    half, near, far = halves(band, nb)
+
+    def arrived(peer):
+        copy_b(lax.rem(band - peer + nb, nb)).wait_recv()
+
     if early:
-        build_table(m_ref, table, nb)
-
-    def done(i, _):
-        copy_b(i).wait()
-        return 0
-
-    lax.fori_loop(1, nb, done, 0)
+        build_table(m_ref, table, signs, nb)
+        for k in range(2):
+            sign[k] = signs[k * half * PR : (k + 1) * half * PR, :].T[:8]
+    build(2)
+    for k in range(1, half):
+        arrived(near + lax.rem(band - near + k, half))
+    if early:
+        left = assemble(out_ref[pl.ds(near, half)], sign[band // half][:1])
+        group = 4
+
+        def synth(c, _):
+            cols = pl.multiple_of(c * (group * BLK), 128)
+            value = jnp.dot(
+                left,
+                table_part(table, near, half, pl.ds(cols, group * BLK)),
+                preferred_element_type=F32,
+            )
+            partial[:, pl.ds(cols, group * BLK)] = value[: 2 * BLK]
+            partial[:, pl.ds(cols + HALF_LON, group * BLK)] = value[2 * BLK :]
+            return 0
+
+        lax.fori_loop(0, XH // group, synth, 0, unroll=XH // group)
+    build(3)
+
+    def done(k, _):
+        arrived(far + k)
+        return 0
+
+    def sent(i, _):
+        copy_b(i).wait_send()
+        return 0
+
+    lax.fori_loop(0, half, done, 0)
+    lax.fori_loop(1, nb, sent, 0)
 
 
 def exchange(temp, surf, legendre, m_order, hydro, coupling, idx, wgt, nb, nl, early):
@@ -361,7 +430,9 @@
         jax.ShapeDtypeStruct((blocks, 2 * HALF, BLK), BF),
     ]
     if early:
-        out_shape.append(jax.ShapeDtypeStruct((nb * PR, NLON), BF))
+        out_shape.append(jax.ShapeDtypeStruct((nb * PR, HALF_LON), BF))
+        out_shape.append(jax.ShapeDtypeStruct((2 * BLK, NLON), F32))
+        out_shape.append(jax.ShapeDtypeStruct((2, 8, nb // 2 * PR), F32))
     return pl.pallas_call(
         functools.partial(exchange_kernel, nb, nl, lat, lev_dev, early),
         out_shape=out_shape,
@@ -381,6 +452,7 @@
             pltpu.VMEM((3, nl * BLK, 2 * BLK), BF),
             pltpu.VMEM((nb + 2 if lat > 16 else 1, PR, 2 * BLK), F32),
             pltpu.VMEM((nb, 2 * PR, BLK), BF),
+            pltpu.VMEM((nb * PR, BLK), F32),
             pltpu.SemaphoreType.DMA((2 * len(CHUNKS),)),
             pltpu.SemaphoreType.DMA((7,)),
             pltpu.SemaphoreType.DMA((len(CHUNKS) * nl,)),
@@ -399,41 +471,43 @@
 
 def grid_kernel(nb, lev_dev, early, src_ref, coef_ref, spread, *refs):
     if early:
-        table, out_ref, src, pool, grid, ss, so = refs
+        table, partial, sign, out_ref, src, pool, grid, ss, so = refs
     else:
-        m_ref, out_ref, src, pool, grid, ss, so, table = refs
-        build_table(m_ref, table, nb)
+        m_ref, out_ref, src, pool, grid, ss, so, table, signs = refs
+        build_table(m_ref, table, signs, nb)
     load_src = pltpu.make_async_copy(src_ref, src, ss)
     load_src.start()
-    coef = coef_ref[...].astype(F32)
-    left = []
-    for p in range(2):
-        tiles = []
-        for b in range(nb):
-            value = coef[b]
-            for r, k in [(r, k) for r in range(2) for k in range(4)] + [(0, 4), (1, 4)]:
-                at = r * PR + k * 2 * Q + p * Q
-                tiles.append(value[at : at + Q])
-        left.append(jnp.concatenate(tiles, axis=0).T)
-    left = jnp.concatenate(left, axis=0).astype(BF)
+    band = lax.axis_index("band")
+    half, _, far = halves(band, nb)
+    if early:
+        left = assemble(coef_ref[pl.ds(far, half)], sign[far // half][:1])
+    else:
+        left = assemble(coef_ref[...], signs[...].T[:1])
     group = 4
 
     def synth(c, _):
-        cols = pl.ds(pl.multiple_of(c * (group * BLK), 128), group * BLK)
-        value = jnp.dot(left, table[:, cols], preferred_element_type=F32).astype(BF)
-        for t in range(3):
-            for p in range(2):
-                at = p * BLK + t * KP
-                for g in range(group):
-                    pool[(2 * t + p) * XB + c * group + g] = value[
-                        at : at + KP, g * BLK : (g + 1) * BLK
-                    ]
-        return 0
-
-    lax.fori_loop(0, XB // group, synth, 0, unroll=XB // group if early else 1)
+        cols = pl.multiple_of(c * (group * BLK), 128)
+        part = pl.ds(cols, group * BLK)
+        part = table_part(table, far, half, part) if early else table[:, part]
+        both = jnp.dot(left, part, preferred_element_type=F32)
+        for side in range(2):
+            value = both[side * 2 * BLK : (side + 1) * 2 * BLK]
+            if early:
+                value = value + partial[:, pl.ds(cols + side * HALF_LON, group * BLK)]
+            value = value.astype(BF)
+            for t in range(3):
+                for p in range(2):
+                    at = p * BLK + t * KP
+                    for g in range(group):
+                        pool[(2 * t + p) * XB + side * XH + c * group + g] = value[
+                            at : at + KP, g * BLK : (g + 1) * BLK
+                        ]
+        return 0
+
+    lax.fori_loop(0, XH // group, synth, 0, unroll=XH // group if early else 1)
     load_src.wait()
 
-    first = (lax.axis_index("band") - 1) * (2 * XB)
+    first = (band - 1) * (2 * XB)
 
     def read(b):
         source = jnp.concatenate([pool[src[i, b] - first] for i in range(4)], axis=1)
@@ -465,10 +539,11 @@
     ]
     src = pltpu.with_memory_space_constraint(src, pltpu.HBM)
     if early:
-        last, specs = list(table), [vmem]
+        last, specs = list(table), [vmem] * len(table)
     else:
         last, specs = [m_order], [pl.BlockSpec(memory_space=pltpu.SMEM)]
-        scratch.append(pltpu.VMEM((nb * PR, NLON), BF))
+        scratch.append(pltpu.VMEM((nb * PR, HALF_LON), BF))
+        scratch.append(pltpu.VMEM((nb * PR, BLK), F32))
     return pl.pallas_call(
         functools.partial(grid_kernel, nb, lev_dev, early),
         out_shape=jax.ShapeDtypeStruct((lev_dev, 2, NLON), F32),

time: 20.7 us -> 19.8 us (0.957)
  Pallas kernels: 20.5 us -> 19.6 us
    pallas_call x1, Pallas kernels: 4.89 us -> 3.82 us  [grid_part(): pl.pallas_call(functools.partial(grid_kernel, nb, lev_dev, early), out_sh...]
where the time goes in v5:
time: 19.8 us; the launch traced here: 19.6 us
  Pallas kernels  19.6 us (99%)
    pallas_call x1, Pallas kernels, exchange(): pl.pallas_call(functools.partial(exchange_kernel, nb, nl, lat, lev_dev, e...  15.8 us
    pallas_call x1, Pallas kernels, grid_part(): pl.pallas_call(functools.partial(grid_kernel, nb, lev_dev, early), out_sh...  3.82 us

profile of v5, /device:TPU:0, one launch (start us, length us, event | category | flops | bytes accessed | tf_op | source)
XLA Modules:
  0.0 19.6 jit_solution(14209141641314897681)
XLA Ops:
  0.0 15.8 %shard_map.91 = (bf16[8,80,128]{2,1,0:T(8,128)(2,1)S(1)}, bf16[80,512,128]{2,1,0:T(8,128)(2,1)S(1)}, bf16[320,2560]{1,0:T(8,128)(2,1)S(1)}, f32[256,5120]{1,0:T(8,128)S(1)}, f32[2,8,160]{2,1,0:T(8,128)S(1)}) custom-call(bf16[20,34,2,1280]{3,2,1,0:T(2,128)(2,1)} %bitcast.5, bf16[20,2,1280]{2,1,0:T(2,128)(2,1)} %bitcast.6, bf16[20,16,1280]{2,1,0:T(8,128)(2,1)} %refs_2_.1, ...), custom_call_target="tpu_custom_call" | custom-call | tf_op jit(solution)/shard_map/pallas_call | solution.py:436
  15.8 3.8 %shard_map.92 = f32[34,2,5120]{2,1,0:T(2,128)} custom-call(s32[4,80]{1,0:T(4,128)} %bitcast.7, bf16[8,80,128]{2,1,0:T(8,128)(2,1)S(1)} %get-tuple-element.10.coef_ref, bf16[80,512,128]{2,1,0:T(8,128)(2,1)S(1)} %get-tuple-element.11.spread, bf16[320,2560]{1,0:T(8,128)(2,1)S(1)} %get-tuple-element.12.refs_0_, f32[256,5120]{1,0:T(8,128)S(1)} %get-tuple-element.13.refs_1_, ...), custom_call_target="tpu_custom_call" | custom-call | tf_op jit(solution)/shard_map/pallas_call | solution.py:547

commit v6 on v5

--- a/solution.py
+++ b/solution.py
@@ -22,8 +22,9 @@
 PR = 40
 JJ = 6
 HALF = 256
-WORK = (10, 40, 30, 0)
-STEP = 5
+WORK = (5, 20, 15, 0)
+KS = 48
+STEP = 10
 MESH = pl.DeviceIdType.MESH
 BF = jnp.bfloat16
 F32 = jnp.float32
@@ -87,17 +88,20 @@
     cells = iota((HALF, BLK), 0).astype(BF)
     zero = jnp.zeros((HALF, BLK), BF)
 
-    def block(b, _):
-        index = idx[b]
-        weight = wgt[b].astype(BF)
-        for h in range(2):
-            spot = (index - h * HALF).astype(F32).astype(BF)
-            total = None
-            for t in range(TAPS):
-                hit = cells == jnp.broadcast_to(spot[t : t + 1, :], (HALF, BLK))
-                part = jnp.where(hit, jnp.broadcast_to(weight[t : t + 1, :], (HALF, BLK)), zero)
-                total = part if total is None else total + part
-            spread[b, h * HALF : (h + 1) * HALF, :] = total
+    def block(x, _):
+        for j in range(2):
+            index = idx[j * XB + x]
+            weight = wgt[j * XB + x].astype(BF)
+            for h in range(2):
+                spot = (index - h * HALF).astype(F32).astype(BF)
+                total = None
+                for t in range(TAPS):
+                    hit = cells == jnp.broadcast_to(spot[t : t + 1, :], (HALF, BLK))
+                    part = jnp.where(
+                        hit, jnp.broadcast_to(weight[t : t + 1, :], (HALF, BLK)), zero
+                    )
+                    total = part if total is None else total + part
+                spread[x, h * HALF : (h + 1) * HALF, j * BLK : (j + 1) * BLK] = total
         return 0
 
     lax.fori_loop(first, last, block, 0)
@@ -190,7 +194,7 @@
     marks = [0]
     for count in WORK:
         marks.append(marks[-1] + count)
-    assert marks[-1] == idx.shape[0]
+    assert 2 * marks[-1] == idx.shape[0]
 
     def build(part):
         build_spread(idx, wgt, spread, marks[part], marks[part + 1])
@@ -427,7 +431,7 @@
     hbm = pl.BlockSpec(memory_space=pltpu.HBM)
     out_shape = [
         jax.ShapeDtypeStruct((nb, 2 * PR, BLK), BF),
-        jax.ShapeDtypeStruct((blocks, 2 * HALF, BLK), BF),
+        jax.ShapeDtypeStruct((blocks // 2, 2 * HALF, 2 * BLK), BF),
     ]
     if early:
         out_shape.append(jax.ShapeDtypeStruct((nb * PR, HALF_LON), BF))
@@ -499,7 +503,7 @@
                 for p in range(2):
                     at = p * BLK + t * KP
                     for g in range(group):
-                        pool[(2 * t + p) * XB + side * XH + c * group + g] = value[
+                        pool[(2 * t + p) * XB + side * XH + c * group + g, :KP] = value[
                             at : at + KP, g * BLK : (g + 1) * BLK
                         ]
         return 0
@@ -509,9 +513,15 @@
 
     first = (band - 1) * (2 * XB)
 
-    def read(b):
-        source = jnp.concatenate([pool[src[i, b] - first] for i in range(4)], axis=1)
-        return jnp.dot(source, spread[b], preferred_element_type=F32)
+    def read(x):
+        source = jnp.concatenate(
+            [
+                jnp.concatenate([pool[src[i, j * XB + x] - first] for i in range(4)], axis=1)
+                for j in range(2)
+            ],
+            axis=0,
+        )
+        return jnp.dot(source, spread[x], preferred_element_type=F32)
 
     def write(q):
         cols = pl.ds(q * (STEP * BLK), STEP * BLK)
@@ -519,8 +529,11 @@
 
     for q in range(XB // STEP):
         for x in range(q * STEP, (q + 1) * STEP):
+            value = read(x)
             for j in range(2):
-                grid[:, j, x * BLK : (x + 1) * BLK] = read(j * XB + x)[:lev_dev]
+                grid[:, j, x * BLK : (x + 1) * BLK] = value[
+                    j * KS : j * KS + lev_dev, j * BLK : (j + 1) * BLK
+                ]
         write(q).start()
     for q in range(XB // STEP):
         write(q).wait()
@@ -532,7 +545,7 @@
     early = len(table) > 0
     scratch = [
         pltpu.SMEM(src.shape, jnp.int32),
-        pltpu.VMEM((JJ * XB, KP, BLK), BF),
+        pltpu.VMEM((JJ * XB, KS, BLK), BF),
         pltpu.VMEM((lev_dev, 2, NLON), F32),
         pltpu.SemaphoreType.DMA,
         pltpu.SemaphoreType.DMA((XB // STEP,)),

time: 19.8 us -> 19.7 us (level)
  no operation moved by 1% of the time
where the time goes in v6:
time: 19.7 us; the launch traced here: 19.6 us
  Pallas kernels  19.5 us (99%)
    pallas_call x1, Pallas kernels, exchange(): pl.pallas_call(functools.partial(exchange_kernel, nb, nl, lat, lev_dev, e...  15.9 us
    pallas_call x1, Pallas kernels, grid_part(): pl.pallas_call(functools.partial(grid_kernel, nb, lev_dev, early), out_sh...  3.66 us

profile of v6, /device:TPU:0, one launch (start us, length us, event | category | flops | bytes accessed | tf_op | source)
XLA Modules:
  0.0 19.6 jit_solution(10474460526482828918)
XLA Ops:
  0.0 15.9 %shard_map.91 = (bf16[8,80,128]{2,1,0:T(8,128)(2,1)S(1)}, bf16[40,512,256]{2,1,0:T(8,128)(2,1)S(1)}, bf16[320,2560]{1,0:T(8,128)(2,1)S(1)}, f32[256,5120]{1,0:T(8,128)S(1)}, f32[2,8,160]{2,1,0:T(8,128)S(1)}) custom-call(bf16[20,34,2,1280]{3,2,1,0:T(2,128)(2,1)} %bitcast.5, bf16[20,2,1280]{2,1,0:T(2,128)(2,1)} %bitcast.6, bf16[20,16,1280]{2,1,0:T(8,128)(2,1)} %refs_2_.1, ...), custom_call_target="tpu_custom_call" | custom-call | tf_op jit(solution)/shard_map/pallas_call | solution.py:440
  15.9 3.7 %shard_map.92 = f32[34,2,5120]{2,1,0:T(2,128)} custom-call(s32[4,80]{1,0:T(4,128)} %bitcast.7, bf16[8,80,128]{2,1,0:T(8,128)(2,1)S(1)} %get-tuple-element.10.coef_ref, bf16[40,512,256]{2,1,0:T(8,128)(2,1)S(1)} %get-tuple-element.11.spread, bf16[320,2560]{1,0:T(8,128)(2,1)S(1)} %get-tuple-element.12.refs_0_, f32[256,5120]{1,0:T(8,128)S(1)} %get-tuple-element.13.refs_1_, ...), custom_call_target="tpu_custom_call" | custom-call | tf_op jit(solution)/shard_map/pallas_call | solution.py:560

commit v7 on v6

--- a/solution.py
+++ b/solution.py
@@ -24,7 +24,7 @@
 HALF = 256
 WORK = (5, 20, 15, 0)
 KS = 48
-STEP = 10
+PARTS = (14, 14, 8, 4)
 MESH = pl.DeviceIdType.MESH
 BF = jnp.bfloat16
 F32 = jnp.float32
@@ -375,14 +375,22 @@
             device_id_type=MESH,
         )
 
-    def send(i, _):
-        copy_b(i).start()
-        return 0
-
-    lax.fori_loop(1, nb, send, 0)
+    half, near, far = halves(band, nb)
+
+    def send(peer):
+        copy_b(lax.rem(peer - band + nb, nb)).start()
+
+    def send_far(k, _):
+        send(far + jnp.where(far > 0, half - 1 - k, k))
+        return 0
+
+    def send_near(k, _):
+        send(near + lax.rem(band - near + k, half))
+        return 0
+
+    lax.fori_loop(0, half, send_far, 0)
+    lax.fori_loop(1, half, send_near, 0)
     out_ref[band] = pieces[band]
-    half, near, far = halves(band, nb)
-
     def arrived(peer):
         copy_b(lax.rem(band - peer + nb, nb)).wait_recv()
 
@@ -524,18 +532,19 @@
         return jnp.dot(source, spread[x], preferred_element_type=F32)
 
     def write(q):
-        cols = pl.ds(q * (STEP * BLK), STEP * BLK)
+        start = sum(PARTS[:q]) * BLK
+        cols = pl.ds(start, PARTS[q] * BLK)
         return pltpu.make_async_copy(grid.at[:, :, cols], out_ref.at[:, :, cols], so.at[q])
 
-    for q in range(XB // STEP):
-        for x in range(q * STEP, (q + 1) * STEP):
+    for q in range(len(PARTS)):
+        for x in range(sum(PARTS[:q]), sum(PARTS[: q + 1])):
             value = read(x)
             for j in range(2):
                 grid[:, j, x * BLK : (x + 1) * BLK] = value[
                     j * KS : j * KS + lev_dev, j * BLK : (j + 1) * BLK
                 ]
         write(q).start()
-    for q in range(XB // STEP):
+    for q in range(len(PARTS)):
         write(q).wait()
 
 
@@ -548,7 +557,7 @@
         pltpu.VMEM((JJ * XB, KS, BLK), BF),
         pltpu.VMEM((lev_dev, 2, NLON), F32),
         pltpu.SemaphoreType.DMA,
-        pltpu.SemaphoreType.DMA((XB // STEP,)),
+        pltpu.SemaphoreType.DMA((len(PARTS),)),
     ]
     src = pltpu.with_memory_space_constraint(src, pltpu.HBM)
     if early:

time: 19.7 us -> 19.6 us (level)
  no operation moved by 1% of the time
where the time goes in v7:
time: 19.6 us; the launch traced here: 19.4 us
  Pallas kernels  19.4 us (99%)
    pallas_call x1, Pallas kernels, exchange(): pl.pallas_call(functools.partial(exchange_kernel, nb, nl, lat, lev_dev, e...  15.8 us
    pallas_call x1, Pallas kernels, grid_part(): pl.pallas_call(functools.partial(grid_kernel, nb, lev_dev, early), out_sh...  3.57 us

profile of v7, /device:TPU:0, one launch (start us, length us, event | category | flops | bytes accessed | tf_op | source)
XLA Modules:
  0.0 19.4 jit_solution(9377587956049631269)
XLA Ops:
  0.0 15.8 %shard_map.91 = (bf16[8,80,128]{2,1,0:T(8,128)(2,1)S(1)}, bf16[40,512,256]{2,1,0:T(8,128)(2,1)S(1)}, bf16[320,2560]{1,0:T(8,128)(2,1)S(1)}, f32[256,5120]{1,0:T(8,128)S(1)}, f32[2,8,160]{2,1,0:T(8,128)S(1)}) custom-call(bf16[20,34,2,1280]{3,2,1,0:T(2,128)(2,1)} %bitcast.5, bf16[20,2,1280]{2,1,0:T(2,128)(2,1)} %bitcast.6, bf16[20,16,1280]{2,1,0:T(8,128)(2,1)} %refs_2_.1, ...), custom_call_target="tpu_custom_call" | custom-call | tf_op jit(solution)/shard_map/pallas_call | solution.py:448
  15.9 3.6 %shard_map.92 = f32[34,2,5120]{2,1,0:T(2,128)} custom-call(s32[4,80]{1,0:T(4,128)} %bitcast.7, bf16[8,80,128]{2,1,0:T(8,128)(2,1)S(1)} %get-tuple-element.10.coef_ref, bf16[40,512,256]{2,1,0:T(8,128)(2,1)S(1)} %get-tuple-element.11.spread, bf16[320,2560]{1,0:T(8,128)(2,1)S(1)} %get-tuple-element.12.refs_0_, f32[256,5120]{1,0:T(8,128)S(1)} %get-tuple-element.13.refs_1_, ...), custom_call_target="tpu_custom_call" | custom-call | tf_op jit(solution)/shard_map/pallas_call | solution.py:569

commit v8 on v7

--- a/solution.py
+++ b/solution.py
@@ -506,14 +506,13 @@
             value = both[side * 2 * BLK : (side + 1) * 2 * BLK]
             if early:
                 value = value + partial[:, pl.ds(cols + side * HALF_LON, group * BLK)]
-            value = value.astype(BF)
             for t in range(3):
                 for p in range(2):
                     at = p * BLK + t * KP
                     for g in range(group):
-                        pool[(2 * t + p) * XB + side * XH + c * group + g, :KP] = value[
-                            at : at + KP, g * BLK : (g + 1) * BLK
-                        ]
+                        pool[(2 * t + p) * XB + side * XH + c * group + g] = value[
+                            at : at + KS, g * BLK : (g + 1) * BLK
+                        ].astype(BF)
         return 0
 
     lax.fori_loop(0, XH // group, synth, 0, unroll=XH // group if early else 1)

time: 19.6 us -> 19.6 us (level)
  no operation moved by 1% of the time
where the time goes in v8:
time: 19.6 us; the launch traced here: 19.4 us
  Pallas kernels  19.4 us (99%)
    pallas_call x1, Pallas kernels, exchange(): pl.pallas_call(functools.partial(exchange_kernel, nb, nl, lat, lev_dev, e...  15.8 us
    pallas_call x1, Pallas kernels, grid_part(): pl.pallas_call(functools.partial(grid_kernel, nb, lev_dev, early), out_sh...  3.57 us

profile of v8, /device:TPU:0, one launch (start us, length us, event | category | flops | bytes accessed | tf_op | source)
XLA Modules:
  0.0 19.4 jit_solution(9758865644864742529)
XLA Ops:
  0.0 15.8 %shard_map.91 = (bf16[8,80,128]{2,1,0:T(8,128)(2,1)S(1)}, bf16[40,512,256]{2,1,0:T(8,128)(2,1)S(1)}, bf16[320,2560]{1,0:T(8,128)(2,1)S(1)}, f32[256,5120]{1,0:T(8,128)S(1)}, f32[2,8,160]{2,1,0:T(8,128)S(1)}) custom-call(bf16[20,34,2,1280]{3,2,1,0:T(2,128)(2,1)} %bitcast.5, bf16[20,2,1280]{2,1,0:T(2,128)(2,1)} %bitcast.6, bf16[20,16,1280]{2,1,0:T(8,128)(2,1)} %refs_2_.1, ...), custom_call_target="tpu_custom_call" | custom-call | tf_op jit(solution)/shard_map/pallas_call | solution.py:448
  15.9 3.6 %shard_map.92 = f32[34,2,5120]{2,1,0:T(2,128)} custom-call(s32[4,80]{1,0:T(4,128)} %bitcast.7, bf16[8,80,128]{2,1,0:T(8,128)(2,1)S(1)} %get-tuple-element.10.coef_ref, bf16[40,512,256]{2,1,0:T(8,128)(2,1)S(1)} %get-tuple-element.11.spread, bf16[320,2560]{1,0:T(8,128)(2,1)S(1)} %get-tuple-element.12.refs_0_, f32[256,5120]{1,0:T(8,128)S(1)} %get-tuple-element.13.refs_1_, ...), custom_call_target="tpu_custom_call" | custom-call | tf_op jit(solution)/shard_map/pallas_call | solution.py:568
